TPU v7x, 512 devices: a whole 4x4x16 slice. The times are simulated.
512 devices in a mesh: rows: 32 (over y_lo, z), cols: 16 (over y_hi, x, core).
Axes of the slice: x: 4, y: 4 (y_hi: 2, y_lo: 2; y = y_hi * 2 + y_lo), z: 16, core: 2. Of those that a mesh axis runs over, the one named last changes fastest.
Arguments:
- latent: bfloat16 [256, 64, 1280], P('rows', 'cols'), may hold values from -6 to 6
- ln_gain: float32 [1, 2, 1280], replicated, may hold values from 0.5 to 1.5
- ln_bias: float32 [1, 2, 1280], replicated, may hold values from -3 to 3
- w_qkv: bfloat16 [1, 1024, 3, 1280], P(None, 'cols'), may hold values from -3 to 3
- w_out: bfloat16 [1, 1024, 1280], P(None, 'cols'), may hold values from -0.375 to 0.375
- w_gate: bfloat16 [1, 1280, 5120], P(None, None, 'cols'), may hold values from -0.15625 to 0.15625
- w_value: bfloat16 [1, 1280, 5120], P(None, None, 'cols'), may hold values from -0.15625 to 0.15625
- w_down: bfloat16 [1, 5120, 1280], P(None, 'cols'), may hold values from -0.078125 to 0.078125
Outputs:
- latent_out: bfloat16 [256, 64, 1280], P('rows', 'cols')
All inputs are finite; a program needn't handle non-finite values.
Results may differ from a plain program's by a relative error of at most 0.023.
Values may be sent and summed in bfloat16 or wider, within the bound.
A program may use at most 64 MiB of HBM per device.

v0:
```python
import math

import jax
import jax.numpy as jnp
from jax import lax
from jax.sharding import PartitionSpec as P

HD = 64
IMG_BITS = 3


def partner(block, axis, distance):
    count = lax.axis_size(axis)
    route = []
    for low in range(count):
        high = low | 1 << distance
        if high != low and high < count:
            route += [(low, high), (high, low)]
    return lax.ppermute(block, axis, route)


def norm_rows(stream, ln_gain, ln_bias):
    values = stream.astype(jnp.float32)
    row_mean = jnp.mean(values, axis=-1, keepdims=True)
    centred = values - row_mean
    row_var = jnp.mean(centred * centred, axis=-1, keepdims=True)
    return (centred * lax.rsqrt(row_var + 1e-05) * ln_gain + ln_bias).astype(jnp.bfloat16)


def collect_image(block):
    position = lax.axis_index("rows")
    for level_bit in range(IMG_BITS):
        other = partner(block, "rows", level_bit)
        upper = position // 2**level_bit % 2 == 1
        block = jnp.where(
            upper, jnp.concatenate([other, block], 0), jnp.concatenate([block, other], 0)
        )
    return block


def attend(packed, head_count):
    local_rows, total_cols = (packed.shape[0], packed.shape[1])
    query_count = local_rows * total_cols
    score_scale = HD ** (-0.5)
    queries = packed[:, :, 0].reshape(query_count, head_count, HD)
    gathered = collect_image(packed[:, :, 1:])
    key_count = gathered.shape[0] * gathered.shape[1]
    block_size = math.gcd(key_count, 1024)
    key_blocks = gathered[:, :, 0].reshape(key_count // block_size, block_size, head_count, HD)
    value_blocks = gathered[:, :, 1].reshape(key_count // block_size, block_size, head_count, HD)

    def fold_keys(running, blocks):
        top_now, mass, accum = running
        key_rows, value_rows = blocks
        scores = (
            jnp.einsum("qhd,khd->hqk", queries, key_rows, preferred_element_type=jnp.float32)
            * score_scale
        )
        new_top = jnp.maximum(top_now, jnp.max(scores, axis=-1))
        weights = jnp.exp(scores - new_top[..., None])
        shrink = jnp.exp(top_now - new_top)
        mass = mass * shrink + jnp.sum(weights, axis=-1)
        accum = accum * shrink[..., None] + jnp.einsum(
            "hqk,khd->hqd",
            weights.astype(jnp.bfloat16),
            value_rows,
            preferred_element_type=jnp.float32,
        )
        return ((new_top, mass, accum), None)

    initial = (
        jnp.full((head_count, query_count), -1e30, jnp.float32),
        jnp.zeros((head_count, query_count), jnp.float32),
        jnp.zeros((head_count, query_count, HD), jnp.float32),
    )
    (top_now, mass, accum), unused = lax.scan(fold_keys, initial, (key_blocks, value_blocks))
    result = (accum / mass[..., None]).transpose(1, 0, 2)
    return result.reshape(local_rows, total_cols, head_count * HD).astype(jnp.bfloat16)


def per_device(latent, ln_gain, ln_bias, w_qkv, w_out, w_gate, w_value, w_down):
    local_rows, local_cols, width = latent.shape
    head_count = w_qkv.shape[1] // HD
    stream = latent
    normed = norm_rows(stream, ln_gain[0, 0], ln_bias[0, 0])
    projection = w_qkv[0]
    packed = jnp.einsum(
        "rwc,etc->rwte",
        lax.all_gather(normed, "cols", axis=1, tiled=True),
        projection,
        preferred_element_type=jnp.float32,
    ).astype(jnp.bfloat16)
    attended = attend(packed, head_count)
    partial_value = jnp.einsum(
        "rwe,ec->rwc", attended, w_out[0], preferred_element_type=jnp.float32
    )
    attn_sum = lax.psum_scatter(
        partial_value.astype(jnp.bfloat16), "cols", scatter_dimension=1, tiled=True
    ).astype(jnp.float32)
    stream = (stream.astype(jnp.float32) + attn_sum).astype(jnp.bfloat16)
    normed_ffn = norm_rows(stream, ln_gain[0, 1], ln_bias[0, 1])
    gate_weight = w_gate[0]
    value_weight = w_value[0]
    down_weight = w_down[0]
    shard_rows = lax.all_gather(normed_ffn, "cols", axis=1, tiled=True)
    token_rows = shard_rows.reshape(-1, width)
    gate_sum = jnp.dot(token_rows, gate_weight, preferred_element_type=jnp.float32)
    value_sum = jnp.dot(token_rows, value_weight, preferred_element_type=jnp.float32)
    hidden = (value_sum * jax.nn.gelu(gate_sum, approximate=False)).astype(jnp.bfloat16)
    terms = jnp.dot(hidden, down_weight, preferred_element_type=jnp.float32)
    ffn_terms = terms.reshape(shard_rows.shape[0], shard_rows.shape[1], width)
    ffn_sum = lax.psum_scatter(
        ffn_terms.astype(jnp.bfloat16), "cols", scatter_dimension=1, tiled=True
    ).astype(jnp.float32)
    stream = (stream.astype(jnp.float32) + ffn_sum).astype(jnp.bfloat16)
    return stream


def solution(mesh):
    return jax.shard_map(
        per_device,
        mesh=mesh,
        in_specs=(
            P("rows", "cols", None),
            P(),
            P(),
            P(None, "cols", None, None),
            P(None, "cols", None),
            P(None, None, "cols"),
            P(None, None, "cols"),
            P(None, "cols", None),
        ),
        out_specs=P("rows", "cols", None),
        check_vma=False,
    )
```

profile of v0, /device:TPU:1, one launch (start us, length us, event | category | flops | bytes accessed | tf_op | source)
XLA Modules:
  0.0 486.3 jit_solution(5928133904377141637)
XLA Ops:
  6.5 1.1 convert_reduce_fusion.1
  7.6 1.1 fusion.48
  8.7 0.8 slice_reduce_fusion
  9.5 1.6 fusion.51
  11.2 67.1 %all-gather.3.cloned.1.call-done = bf16[8,64,1280]{2,0,1:T(8,128)(2,1)} async-done(((bf16[8,4,1280]{2,0,1:T(8,128)(2,1)}), bf16[8,64,1280]{2,0,1:T(8,128)(2,1)}) %all-gather.3.cloned.1.call-update) | async-done | bytes 1310736 | tf_op jit(solution)/shard_map/all_gather | solution.py:89
  78.4 3.0 fusion.23
  81.4 1.0 slice.32
  82.3 3.2 collective-permute-start
  85.6 6.3 %collective-permute-done = bf16[8,64,2,64]{3,1,2,0:T(8,128)(2,1)S(1)} collective-permute-done((bf16[8,64,2,64]{3,1,2,0:T(8,128)(2,1)S(1)}, bf16[8,64,2,64]{3,1,2,0:T(8,128)(2,1)S(1)}, u32[]{:S(2)}, u32[]{:S(2)}) %collective-permute-start) | collective-permute-done | bytes 131104 | tf_op jit(solution)/shard_map/ppermute | solution.py:19
  91.9 0.2 maximum_select_fusion.2
  92.1 4.2 collective-permute-start.1
  96.3 22.6 %collective-permute-done.1 = bf16[16,64,2,64]{3,1,2,0:T(8,128)(2,1)S(1)} collective-permute-done((bf16[16,64,2,64]{3,1,2,0:T(8,128)(2,1)S(1)}, bf16[16,64,2,64]{3,1,2,0:T(8,128)(2,1)S(1)}, u32[]{:S(2)}, u32[]{:S(2)}) %collective-permute-start.1) | collective-permute-done | bytes 262176 | tf_op jit(solution)/shard_map/ppermute | solution.py:19
  118.9 0.4 maximum_select_fusion.1
  119.4 7.4 %collective-permute-start.2 = (bf16[32,64,2,64]{3,1,2,0:T(8,128)(2,1)S(1)}, bf16[32,64,2,64]{3,1,2,0:T(8,128)(2,1)S(1)}, u32[]{:S(2)}, u32[]{:S(2)}) collective-permute-start(bf16[32,64,2,64]{3,1,2,0:T(8,128)(2,1)S(1)} %maximum_select_fusion.1), channel_id=1, source_target_pairs={{0,64},{64,0},{16,80},{80,16},{32,96},{96,32},{48,112},{112,48},{1... | collective-permute-start | bytes 1572872 | tf_op jit(solution)/shard_map/ppermute | solution.py:19
  126.8 0.9 slice.34
  127.9 88.9 %collective-permute-done.2 = bf16[32,64,2,64]{3,1,2,0:T(8,128)(2,1)S(1)} collective-permute-done((bf16[32,64,2,64]{3,1,2,0:T(8,128)(2,1)S(1)}, bf16[32,64,2,64]{3,1,2,0:T(8,128)(2,1)S(1)}, u32[]{:S(2)}, u32[]{:S(2)}) %collective-permute-start.2) | collective-permute-done | bytes 524320 | tf_op jit(solution)/shard_map/ppermute | solution.py:19
  216.8 0.9 maximum_select_fusion
  217.7 0.2 fusion.56
  217.9 1.1 copy.33
  219.0 0.3 copy.31
  219.3 9.4 %while.15 = (s32[]{:T(128)}, f32[1,512]{1,0:T(1,128)S(1)}, f32[1,512]{1,0:T(1,128)S(1)}, f32[1,512,64]{1,2,0:T(8,128)S(1)}, bf16[4,1024,1,64]{1,3,2,0:T(8,128)(2...) while((s32[]{:T(128)}, f32[1,512]{1,0:T(1,128)S(1)}, ...), condition=%wide.region_5.6_spmd.clone, body=%wide.region_2.5_spmd.clone.sunk | while | flops 138512896 | bytes 6914169 | solution.py:76
  219.3 0.5 multiply_reduce_fusion.2
  219.8 0.4 fusion.70
  220.3 1.4 fusion.72
  221.7 0.5 multiply_reduce_fusion.2
  222.2 0.4 fusion.70
  222.6 1.4 fusion.72
  224.0 0.5 multiply_reduce_fusion.2
  224.5 0.4 fusion.70
  224.9 1.4 fusion.72
  226.4 0.5 multiply_reduce_fusion.2
  226.9 0.4 fusion.70
  227.3 1.4 fusion.72
  228.9 0.5 convolution_convert_fusion.1
  229.3 1.8 copy.35
  231.2 86.2 %reduce-scatter.3.cloned.1.call-done = bf16[8,4,1280]{2,0,1:T(8,128)(2,1)} async-done(((bf16[8,64,1280]{2,0,1:T(8,128)(2,1)}), bf16[8,4,1280]{2,0,1:T(8,128)(2,1)}) %reduce-scatter.3.cloned.1.call-update) | async-done | bytes 81936 | tf_op jit(solution)/shard_map/reduce_scatter | solution.py:97
  317.5 1.0 convert_reduce_fusion
  318.6 0.7 fusion.47
  319.5 64.2 %all-gather.5.cloned.1.call-done = bf16[8,64,1280]{2,0,1:T(8,128)(2,1)} async-done(((bf16[8,4,1280]{2,0,1:T(8,128)(2,1)}), bf16[8,64,1280]{2,0,1:T(8,128)(2,1)}) %all-gather.5.cloned.1.call-update) | async-done | bytes 1310736 | tf_op jit(solution)/shard_map/all_gather | solution.py:105
  383.6 1.5 copy.36
  385.2 0.6 fusion.27
  385.8 1.9 fusion.22
  387.7 0.2 copy.37
  387.9 0.8 convolution_convert_fusion
  388.7 1.8 copy.38
  390.6 87.6 %reduce-scatter.5.cloned.1.call-done = bf16[8,4,1280]{2,0,1:T(8,128)(2,1)} async-done(((bf16[8,64,1280]{2,0,1:T(8,128)(2,1)}), bf16[8,4,1280]{2,0,1:T(8,128)(2,1)}) %reduce-scatter.5.cloned.1.call-update) | async-done | bytes 81936 | tf_op jit(solution)/shard_map/reduce_scatter | solution.py:112
  478.2 0.9 fusion.53
  479.1 0.7 copy.39
  (41 shorter events, 0.8 us)
Async XLA Ops:
  6.5 381.4 %copy-start = (bf16[1,320,1280]{2,1,0:T(8,128)(2,1)S(1)}, bf16[1,320,1280]{2,1,0:T(8,128)(2,1)}, u32[]{:S(2)}) copy-start(bf16[1,320,1280]{2,1,0:T(8,128)(2,1)} %param.17) | copy-start | bytes 2457604
  6.5 71.8 %all-gather.3.cloned.1.call-start = ((), (), s32[]{:S(2)}) async-start(), calls=%async_computation.2 | async-start | bytes 1392640 | tf_op jit(solution)/shard_map/all_gather | solution.py:89
  11.2 306.3 %reduce-scatter.3.cloned.1.call-start = ((), (), s32[]{:S(2)}) async-start(), calls=%async_computation.3 | async-start | bytes 1392640 | tf_op jit(solution)/shard_map/reduce_scatter | solution.py:97
  82.3 9.5 %collective-permute-start = (bf16[8,64,2,64]{3,1,2,0:T(8,128)(2,1)S(1)}, bf16[8,64,2,64]{3,1,2,0:T(8,128)(2,1)S(1)}, u32[]{:S(2)}, u32[]{:S(2)}) collective-permute-start(bf16[8,64,2,64]{3,1,2,0:T(8,128)(2,1)S(1)} %slice.32), channel_id=1, source_target_pairs={{0,16},{16,0},{32,48},{48,32},{64,80},{80,64},{96,112},{112,96},{1... | collective-permute-start | bytes 393224 | tf_op jit(solution)/shard_map/ppermute | solution.py:19
  92.1 26.8 %collective-permute-start.1 = (bf16[16,64,2,64]{3,1,2,0:T(8,128)(2,1)S(1)}, bf16[16,64,2,64]{3,1,2,0:T(8,128)(2,1)S(1)}, u32[]{:S(2)}, u32[]{:S(2)}) collective-permute-start(bf16[16,64,2,64]{3,1,2,0:T(8,128)(2,1)S(1)} %maximum_select_fusion.2), channel_id=1, source_target_pairs={{0,32},{32,0},{16,48},{48,16},{64,96},{96,64},{80,112},{112,80},{1... | collective-permute-start | bytes 786440 | tf_op jit(solution)/shard_map/ppermute | solution.py:19
  119.4 97.4 %collective-permute-start.2 = (bf16[32,64,2,64]{3,1,2,0:T(8,128)(2,1)S(1)}, bf16[32,64,2,64]{3,1,2,0:T(8,128)(2,1)S(1)}, u32[]{:S(2)}, u32[]{:S(2)}) collective-permute-start(bf16[32,64,2,64]{3,1,2,0:T(8,128)(2,1)S(1)} %maximum_select_fusion.1), channel_id=1, source_target_pairs={{0,64},{64,0},{16,80},{80,16},{32,96},{96,32},{48,112},{112,48},{1... | collective-permute-start | bytes 1572872 | tf_op jit(solution)/shard_map/ppermute | solution.py:19
  219.3 9.5 %copy-start.2 = (bf16[1,64,1280]{2,1,0:T(8,128)(2,1)S(1)}, bf16[1,64,1280]{2,1,0:T(8,128)(2,1)}, u32[]{:S(2)}) copy-start(bf16[1,64,1280]{2,1,0:T(8,128)(2,1)} %param.14) | copy-start | bytes 491524
  229.3 88.1 %copy-start.1 = (bf16[8,4,1280]{2,1,0:T(4,128)(2,1)S(1)}, bf16[8,4,1280]{2,1,0:T(4,128)(2,1)}, u32[]{:S(2)}) copy-start(bf16[8,4,1280]{2,1,0:T(4,128)(2,1)} %param.10) | copy-start | bytes 245764
  231.1 154.0 %copy-start.3 = (bf16[1,1280,320]{1,2,0:T(8,128)(2,1)S(1)}, bf16[1,1280,320]{1,2,0:T(8,128)(2,1)}, u32[]{:S(2)}) copy-start(bf16[1,1280,320]{1,2,0:T(8,128)(2,1)} %param.15) | copy-start | bytes 2457604
  231.2 152.5 %all-gather.5.cloned.1.call-start = ((), (), s32[]{:S(2)}) async-start(), calls=%async_computation.4 | async-start | bytes 1392640 | tf_op jit(solution)/shard_map/all_gather | solution.py:105
  319.4 66.4 %copy-start.4 = (bf16[1,1280,320]{1,2,0:T(8,128)(2,1)S(1)}, bf16[1,1280,320]{1,2,0:T(8,128)(2,1)}, u32[]{:S(2)}) copy-start(bf16[1,1280,320]{1,2,0:T(8,128)(2,1)} %param.16) | copy-start | bytes 2457604
  319.4 158.8 %reduce-scatter.5.cloned.1.call-start = ((), (), s32[]{:S(2)}) async-start(), calls=%async_computation.5 | async-start | bytes 1392640 | tf_op jit(solution)/shard_map/reduce_scatter | solution.py:112
Sparse Core Ops, SparseCore 0:
  11.3 67.0 all-gather.2
  231.3 86.1 reduce-scatter.2
  320.8 62.8 all-gather.4
  390.7 87.4 reduce-scatter.4
where the time goes:
time: 488 us; the launch traced here: 486 us
  waiting for transfers between devices  423 us (87%)
  starting transfers between devices  14.9 us (3%)
  matrix products  14.3 us (3%)
  between operations  13.4 us (3%)
  local copies, waits for them, and re-layouts  10.6 us (2%)
  other arithmetic  9.85 us (2%)
    ppermute x3, waiting for transfers between devices, partner(): return lax.ppermute(block, axis, route)  118 us
    reduce_scatter x1, waiting for transfers between devices, per_device(): lax.psum_scatter(ffn_terms.astype(jnp.bfloat16), 'cols', scatter_dimensio...  87.6 us
    reduce_scatter x1, waiting for transfers between devices, per_device(): lax.psum_scatter(partial_value.astype(jnp.bfloat16), 'cols', scatter_dime...  86.2 us
    all_gather x1, waiting for transfers between devices, per_device(): lax.all_gather(normed, 'cols', axis=1, tiled=True)  67.1 us
    all_gather x1, waiting for transfers between devices, per_device(): shard_rows = lax.all_gather(normed_ffn, 'cols', axis=1, tiled=True)  64.2 us
    ppermute x3, starting transfers between devices, partner(): return lax.ppermute(block, axis, route)  14.8 us
  transfers between devices with their start and end apart: 7, of which 7 were waited for; matrix products, arithmetic and copies ran while one was open for 0% of the time, Pallas kernels for 0%

commit v1 on v0

v1 whole, which is shorter than its diff:
```python
import math

import jax
import jax.numpy as jnp
from jax import lax
from jax.experimental import pallas as pl
from jax.experimental.pallas import tpu as pltpu
from jax.sharding import PartitionSpec as P

HD = 64
MESH = pl.DeviceIdType.MESH
F32, BF16 = jnp.float32, jnp.bfloat16
ORDERS = ((1, 2, 3, 7, 6, 5, 4), (2, 0, 3, 7, 6, 5, 4), (3, 1, 7, 0, 6, 5, 4), (7, 2, 6, 1, 5, 0, 4))
CODES = [sum(digit * 8**place for place, digit in enumerate(order)) for order in ORDERS]


def norm_rows(values, gain, bias):
    row_mean = jnp.mean(values, axis=-1, keepdims=True)
    centred = values - row_mean
    row_var = jnp.mean(centred * centred, axis=-1, keepdims=True)
    return (centred * lax.rsqrt(row_var + 1e-05) * gain + bias).astype(BF16)


def dot(left, right, left_dim, right_dim):
    return lax.dot_general(
        left, right, (((left_dim,), (right_dim,)), ((), ())), preferred_element_type=F32
    )


def block_kernel(
    latent, gain, bias, w_qkv, w_out, w_gate, w_value, w_down, result,
    gathered, partial, summed, keys, other_keys, query, wkv, wq, wo, wgv, wdown,
    top, accum, attended, attended_other, query_other, hidden,
    sem_w, sem_ws, sem_wr, sem_cs, sem_cr, sem_z, sem_zs, sem_sib, sem_sibs, sem_p, sem_ps,
):
    row, col = lax.axis_index("rows"), lax.axis_index("cols")
    core = col % 2
    place = row % 8
    half = place // 4
    jj = place + half * (7 - 2 * place)
    step = 1 - 2 * half
    inward, outward = row + step, row - step
    entry = row - place + 4 - half
    sibling = (row, col + 1 - 2 * core)
    across = (row + 4 - 8 * half, col)
    mate = lax.bitwise_xor(core, half)

    def chip(distance):
        return (row, lax.bitwise_xor(col, 2 * distance))

    barrier = pltpu.get_barrier_semaphore()
    for distance in range(1, 8):
        pl.semaphore_signal(barrier, inc=1, device_id=chip(distance), device_id_type=MESH)
        pl.semaphore_signal(
            barrier, inc=1, device_id=(lax.bitwise_xor(row, distance), col), device_id_type=MESH
        )
    pl.semaphore_signal(barrier, inc=1, device_id=sibling, device_id_type=MESH)
    pl.semaphore_wait(barrier, 15)

    started = []

    def remote(src, dst, send, recv, device):
        return pltpu.make_async_remote_copy(
            src_ref=src, dst_ref=dst, send_sem=send, recv_sem=recv, device_id=device, device_id_type=MESH
        )

    def begin(*args):
        copy = remote(*args)
        copy.start()
        started.append(copy)
        return copy

    weights = []

    def load_weight(index, src, dst_mine, dst_theirs):
        own = pltpu.make_async_copy(src, dst_mine, sem_w.at[index])
        own.start()
        weights.append((own, begin(src, dst_theirs, sem_ws.at[index], sem_wr.at[index], sibling)))

    load_weight(0, w_qkv.at[pl.ds(HD, 2 * HD)], wkv.at[mate], wkv.at[mate])
    load_weight(1, w_qkv.at[pl.ds(0, HD)], wq.at[mate], wq.at[mate])

    def exchange(buffer, target, first, same):
        copies = []
        for distance in range(1, 8):
            src = buffer.at[0] if same else buffer.at[distance]
            copies.append(
                begin(src, target.at[distance], sem_cs.at[first, distance], sem_cr.at[first, distance], chip(distance))
            )
        return copies

    stream = latent[...].astype(F32)
    gathered[0, 0] = norm_rows(stream, gain[0:1, :], bias[0:1, :])
    copies = exchange(gathered.at[0], gathered.at[0], 0, True)

    load_weight(2, w_out, wo.at[mate], wo.at[mate])
    load_weight(3, w_gate, wgv.at[0], wgv.at[1])
    load_weight(4, w_value, wgv.at[2], wgv.at[3])
    load_weight(5, w_down, wdown.at[0], wdown.at[1])

    for own, sent in weights[:2]:
        own.wait()
        sent.wait_recv()
    for copy in copies:
        copy.wait_recv()

    tokens = gathered[0].reshape(256, -1)
    scale = HD ** (-0.5) * math.log2(math.e)
    queries = (dot(wq[...].reshape(2 * HD, -1), tokens, 1, 1) * scale).astype(BF16)
    query_other[...] = queries[HD:]
    send_query = begin(
        query_other, query.at[pl.ds(0, HD), pl.ds(256, 256)], sem_ps.at[0], sem_p.at[0], across
    )
    packed = dot(tokens, wkv[...].reshape(4 * HD, -1), 1, 1).astype(BF16)
    other_keys[...] = packed[:, 2 * HD :]
    keys[jj, core] = packed[:, : 2 * HD]
    send_foreign = remote(
        other_keys, keys.at[4 + jj, core], sem_ps.at[1], sem_z.at[4 + jj], (entry, col)
    )
    send_foreign.start()
    own_keys = keys.at[jj, core]

    def send_inward(origin, send):
        block = keys.at[origin, core]
        return remote(block, block, send, sem_z.at[origin], (inward, col))

    def send_outward(origin, send):
        block = keys.at[origin, core]
        return remote(block, block, send, sem_z.at[origin], (outward, col))

    def send_sibling(origin):
        block = keys.at[origin, core]
        return remote(block, block, sem_sibs.at[origin], sem_sib.at[origin], sibling)

    def from_sibling(origin):
        block = keys.at[origin, 1 - core]
        return remote(block, block, sem_sibs.at[origin], sem_sib.at[origin], sibling)

    @pl.when(jj >= 1)
    def _():
        send_outward(jj, sem_ps.at[2]).start()

    @pl.when(jj <= 2)
    def _():
        send_inward(jj, sem_ps.at[3]).start()

    send_sibling(jj).start()
    query[0:HD, 0:256] = queries[:HD]
    query[HD:, :] = jnp.zeros((HD, 512), BF16)
    top[...] = jnp.full(top.shape, -1e30, F32)
    accum[...] = jnp.zeros(accum.shape, F32)
    ones_lane = lax.broadcasted_iota(jnp.int32, (512, 2 * HD), 1) < HD

    def fold(origin):
        from_sibling(origin).wait_recv()
        block = keys[origin].reshape(512, 2 * HD)
        scores = dot(block, query[...], 1, 0)
        old = top[...]
        new = jnp.maximum(old, jnp.max(scores, axis=0, keepdims=True))
        weights_ = jnp.exp2(scores - new).astype(BF16)
        values = jnp.where(ones_lane, jnp.ones_like(block), block)
        accum[...] = accum[...] * jnp.exp2(old - new) + dot(values, weights_, 0, 0)
        top[...] = new

    is0 = (1 - jj) * (2 - jj) * (3 - jj) // 6
    is1 = jj * (2 - jj) * (3 - jj) // 2
    is2 = jj * (jj - 1) * (3 - jj) // 2
    is3 = jj * (jj - 1) * (jj - 2) // 6
    code = is0 * CODES[0] + is1 * CODES[1] + is2 * CODES[2] + is3 * CODES[3]

    def one_step(index, carry):
        rest, before = carry
        origin = rest % 8
        send_outward(origin, sem_zs.at[origin]).wait_recv()

        @pl.when(jnp.logical_and(origin > jj, jj >= 1))
        def _():
            send_outward(origin, sem_zs.at[origin]).start()

        @pl.when(jnp.logical_and(origin < jj, jj <= 2))
        def _():
            send_inward(origin, sem_zs.at[origin]).start()

        send_sibling(origin).start()
        fold(before)
        return (rest // 8, origin)

    send_query.wait_recv()
    _, last = lax.fori_loop(0, 7, one_step, (code, jj))
    fold(last)

    def finish_step(origin, carry):
        send_sibling(origin).wait_send()

        @pl.when(
            jnp.logical_or(
                jnp.logical_and(origin > jj, jj >= 1), jnp.logical_and(origin < jj, jj <= 2)
            )
        )
        def _():
            send_outward(origin, sem_zs.at[origin]).wait_send()

        return carry

    final = (accum[HD:, :] / accum[0:1, :]).astype(BF16)
    attended_other[...] = final[:, 256:]
    send_attended = begin(
        attended_other, attended.at[pl.ds(HD, HD)], sem_ps.at[4], sem_p.at[1], across
    )
    attended[0:HD, :] = final[:, :256]
    for own, sent in weights[2:]:
        own.wait()
        sent.wait_recv()
    send_attended.wait_recv()
    partial[0] = (
        dot(attended[...], wo[...].reshape(2 * HD, -1), 0, 0).astype(BF16).reshape(partial.shape[1:])
    )
    copies = exchange(partial.at[0], summed.at[0], 1, False)
    total = stream + partial[0, 0].astype(F32)
    for distance, copy in enumerate(copies):
        copy.wait_recv()
        total += summed[0, distance + 1].astype(F32)
    stream = total.astype(BF16).astype(F32)

    gathered[1, 0] = norm_rows(stream, gain[1:2, :], bias[1:2, :])
    copies = exchange(gathered.at[1], gathered.at[1], 2, True)
    for copy in copies:
        copy.wait_recv()
    tokens = gathered[1].reshape(256, -1)
    units = wdown.shape[0] * wdown.shape[1]
    sums = dot(tokens, wgv[...].reshape(2 * units, -1), 1, 1)
    gate, value = sums[:, :units], sums[:, units:]
    hidden[...] = (value * (gate * (lax.erf(gate * (0.5**0.5)) + 1.0) * 0.5)).astype(BF16)
    terms = dot(hidden[...], wdown[...].reshape(units, -1), 1, 0)
    partial[1] = terms.astype(BF16).reshape(partial.shape[1:])
    copies = exchange(partial.at[1], summed.at[1], 3, False)
    total = stream + partial[1, 0].astype(F32)
    for distance, copy in enumerate(copies):
        copy.wait_recv()
        total += summed[1, distance + 1].astype(F32)
    result[...] = total.astype(BF16)

    for copy in started:
        copy.wait_send()
    send_foreign.wait_send()

    @pl.when(jj >= 1)
    def _():
        send_outward(jj, sem_ps.at[2]).wait_send()

    @pl.when(jj <= 2)
    def _():
        send_inward(jj, sem_ps.at[3]).wait_send()

    lax.fori_loop(0, 8, finish_step, 0)


def per_device(latent, ln_gain, ln_bias, w_qkv, w_out, w_gate, w_value, w_down):
    width = latent.shape[-1]
    own_rows = w_gate.shape[2]
    vmem, anywhere = pl.BlockSpec(memory_space=pltpu.VMEM), pl.BlockSpec(memory_space=pl.ANY)
    dma = pltpu.SemaphoreType.DMA
    stream = pl.pallas_call(
        block_kernel,
        out_shape=jax.ShapeDtypeStruct((32, width), BF16),
        in_specs=[vmem] * 3 + [anywhere] * 5,
        out_specs=vmem,
        scratch_shapes=[
            pltpu.VMEM((2, 8, 32, width), BF16),
            pltpu.VMEM((2, 8, 32, width), BF16),
            pltpu.VMEM((2, 8, 32, width), BF16),
            pltpu.VMEM((8, 2, 256, 2 * HD), BF16),
            pltpu.VMEM((256, 2 * HD), BF16),
            pltpu.VMEM((2 * HD, 512), BF16),
            pltpu.VMEM((2, 2 * HD, width), BF16),
            pltpu.VMEM((2, HD, width), BF16),
            pltpu.VMEM((2, HD, width), BF16),
            pltpu.VMEM((4, own_rows, width), BF16),
            pltpu.VMEM((2, own_rows, width), BF16),
            pltpu.VMEM((1, 512), F32),
            pltpu.VMEM((2 * HD, 512), F32),
            pltpu.VMEM((2 * HD, 256), BF16),
            pltpu.VMEM((HD, 256), BF16),
            pltpu.VMEM((HD, 256), BF16),
            pltpu.VMEM((256, 2 * own_rows), BF16),
            dma((6,)),
            dma((6,)),
            dma((6,)),
            dma((4, 8)),
            dma((4, 8)),
            dma((8,)),
            dma((8,)),
            dma((8,)),
            dma((8,)),
            dma((2,)),
            dma((5,)),
        ],
        compiler_params=pltpu.CompilerParams(
            collective_id=0, has_side_effects=True, vmem_limit_bytes=56 * 2**20
        ),
        name="transformer_block",
    )(
        latent.reshape(32, width),
        ln_gain[0],
        ln_bias[0],
        w_qkv[0].transpose(1, 0, 2).reshape(3 * HD, width),
        w_out[0],
        w_gate[0].T,
        w_value[0].T,
        w_down[0],
    )
    return stream.reshape(latent.shape)


def solution(mesh):
    return jax.shard_map(
        per_device,
        mesh=mesh,
        in_specs=(
            P("rows", "cols", None),
            P(),
            P(),
            P(None, "cols", None, None),
            P(None, "cols", None),
            P(None, None, "cols"),
            P(None, None, "cols"),
            P(None, "cols", None),
        ),
        out_specs=P("rows", "cols", None),
        check_vma=False,
    )
```

time: 488 us -> 93.5 us (0.19)
  waiting for transfers between devices: 423 us -> 0 us
  Pallas kernels: 0 us -> 89.9 us
  starting transfers between devices: 14.9 us -> 0 us
  matrix products: 14.3 us -> 0 us
  between operations: 13.4 us -> 0.01 us
  other arithmetic: 9.85 us -> 0 us
  local copies, waits for them, and re-layouts: 10.6 us -> 3.09 us
    reduce_scatter x2 -> x0, waiting for transfers between devices: 174 us -> none  [the longest x1 87.6 us: per_device(): lax.psum_scatter(ffn_terms.astype(jnp.bfloat16), 'cols', scatter_dimensio...]
    all_gather x2 -> x0, waiting for transfers between devices: 131 us -> none  [the longest x1 67.1 us: per_device(): lax.all_gather(normed, 'cols', axis=1, tiled=True)]
    ppermute x3 -> x0, waiting for transfers between devices: 118 us -> none  [partner(): return lax.ppermute(block, axis, route)]
    pallas_call x0 -> x1, Pallas kernels: none -> 89.9 us  [per_device(): pl.pallas_call(block_kernel, out_shape=jax.ShapeDtypeStruct((32, width),...]
    ppermute x3 -> x0, starting transfers between devices: 14.8 us -> none  [partner(): return lax.ppermute(block, axis, route)]
    dot_general x13 -> x0, matrix products: 14.3 us -> none  [the longest x4 5.56 us: fold_keys(): jnp.einsum('hqk,khd->hqd', weights.astype(jnp.bfloat16), value_rows, pref...]
    reduce_sum x8 -> x0, other arithmetic: 4.88 us -> none  [the longest x2 2.05 us: norm_rows(): row_mean = jnp.mean(values, axis=-1, keepdims=True)]
  transfers between devices with their start and end apart: 7 -> 0, of which waited for: 7 -> 0; matrix products, arithmetic and copies ran while one was open for 0% -> 0% of each run, Pallas kernels for 0% -> 0%
where the time goes in v1:
time: 93.5 us; the launch traced here: 93 us
  Pallas kernels  89.9 us (96%)
  local copies, waits for them, and re-layouts  3.09 us (3%)
    pallas_call x1, Pallas kernels, per_device(): pl.pallas_call(block_kernel, out_shape=jax.ShapeDtypeStruct((32, width),...  89.9 us

profile of v1, /device:TPU:1, one launch (start us, length us, event | category | flops | bytes accessed | tf_op | source)
XLA Modules:
  0.0 93.0 jit_solution(8223710201140604683)
XLA Ops:
  0.0 1.5 %reshape.9.latent = bf16[32,1280]{1,0:T(8,128)(2,1)} reshape(bf16[8,4,1280]{2,1,0:T(4,128)(2,1)} %param.8) | data formatting | bytes 163840 | tf_op jit(solution)/shard_map/reshape | solution.py:303
  1.5 89.9 %transformer_block.1 = bf16[32,1280]{1,0:T(8,128)(2,1)} custom-call(bf16[32,1280]{1,0:T(8,128)(2,1)} %reshape.9.latent, f32[2,1280]{1,0:T(2,128)} %bitcast.20, f32[2,1280]{1,0:T(2,128)} %bitcast.21, bf16[192,1280]{1,0:T(8,128)(2,1)} %bitcast.18, bf16[64,1280]{1,0:T(8,128)(2,1)} %bitcast.19, bf16[320,1280]{1,0:T(8,128)(2,1)} %bitcast.15, ...), custom_call_target="tpu_custom_call" | custom-call | tf_op jit(solution)/shard_map/transformer_block/pallas_call | solution.py:263
  91.5 1.5 %reshape.11 = bf16[8,4,1280]{2,1,0:T(4,128)(2,1)} reshape(bf16[32,1280]{1,0:T(8,128)(2,1)} %transformer_block.1) | data formatting | bytes 163840 | tf_op jit(solution)/shard_map/reshape | solution.py:312

commit v2 on v0

v2 whole, which is shorter than its diff:
```python
import math

import jax
import jax.numpy as jnp
from jax import lax
from jax.experimental import pallas as pl
from jax.experimental.pallas import tpu as pltpu
from jax.sharding import PartitionSpec as P

HD = 64
MESH = pl.DeviceIdType.MESH
F32, BF16 = jnp.float32, jnp.bfloat16


def norm_rows(values, gain, bias):
    row_mean = jnp.mean(values, axis=-1, keepdims=True)
    centred = values - row_mean
    row_var = jnp.mean(centred * centred, axis=-1, keepdims=True)
    return (centred * lax.rsqrt(row_var + 1e-05) * gain + bias).astype(BF16)


def dot(left, right, left_dim, right_dim):
    return lax.dot_general(
        left, right, (((left_dim,), (right_dim,)), ((), ())), preferred_element_type=F32
    )


def block_kernel(
    latent, gain, bias, w_qkv, w_out, w_gate, w_value, w_down, result,
    rows_in, tokens, stream, partial, summed, keys, other_keys, query, query_other,
    wkv, wq, wo, wgv, wdown, top, accum, attended, attended_other,
    sem_w, sem_ws, sem_wr, sem_os, sem_or, sem_fs, sem_fr, sem_xs, sem_xr,
    sem_as, sem_ar, sem_zs, sem_zr, sem_gs, sem_cs, sem_cr, sem_ps, sem_pr,
):
    row, col = lax.axis_index("rows"), lax.axis_index("cols")
    core, me = col % 2, col // 2
    mate = lax.bitwise_xor(core, row % 8 // 4)
    sibling = (row, col + 1 - 2 * core)

    def chip(distance):
        return (row, lax.bitwise_xor(col, 2 * distance))

    def plane(distance):
        return (lax.bitwise_xor(row, distance), col)

    def remote(src, dst, send, recv, device):
        return pltpu.make_async_remote_copy(
            src_ref=src, dst_ref=dst, send_sem=send, recv_sem=recv, device_id=device, device_id_type=MESH
        )

    started = []

    def begin(*args):
        copy = remote(*args)
        copy.start()
        started.append(copy)
        return copy

    barrier = pltpu.get_barrier_semaphore()
    for distance in range(1, 8):
        pl.semaphore_signal(barrier, inc=1, device_id=chip(distance), device_id_type=MESH)
    for distance in range(1, 5):
        pl.semaphore_signal(barrier, inc=1, device_id=plane(distance), device_id_type=MESH)
    pl.semaphore_signal(barrier, inc=1, device_id=sibling, device_id_type=MESH)
    pl.semaphore_wait(barrier, 12)

    for distance in range(7, 0, -1):
        begin(latent, rows_in.at[me], sem_xs.at[distance], sem_xr.at[distance], chip(distance))
    rows_in[me] = latent[...]
    weights = []

    def load_weight(index, src, mine, theirs):
        own = pltpu.make_async_copy(src, mine, sem_w.at[index])
        own.start()
        weights.append((own, begin(src, theirs, sem_ws.at[index], sem_wr.at[index], sibling)))

    load_weight(0, w_qkv.at[pl.ds(HD, 2 * HD)], wkv.at[mate], wkv.at[mate])
    load_weight(1, w_qkv.at[pl.ds(0, HD)], wq.at[mate], wq.at[mate])
    load_weight(2, w_out, wo.at[0, mate], wo.at[0, mate])
    load_weight(3, w_gate, wgv.at[0], wgv.at[1])
    load_weight(4, w_value, wgv.at[2], wgv.at[3])
    load_weight(5, w_down, wdown.at[0], wdown.at[1])

    def rows_copy(distance):
        return remote(
            latent, rows_in.at[lax.bitwise_xor(me, distance)], sem_xs.at[distance], sem_xr.at[distance], chip(distance)
        )

    def first_norm(index, carry):
        slot = lax.bitwise_xor(me, index)

        @pl.when(index >= 1)
        def _():
            rows_copy(index).wait_recv()

        tokens[slot] = norm_rows(rows_in[slot].astype(F32), gain[0:1, :], bias[0:1, :])
        return carry

    lax.fori_loop(0, 8, first_norm, 0)
    for own, sent in weights[:2]:
        own.wait()
        sent.wait_recv()

    every = tokens[...].reshape(256, -1)
    packed = dot(every, wkv[...].reshape(4 * HD, -1), 1, 1).astype(BF16)
    other_keys[...] = packed[:, 2 * HD :]
    begin(other_keys, keys.at[4, core], sem_zs.at[4], sem_zr.at[4], plane(4))
    scale = HD ** (-0.5) * math.log2(math.e)
    queries = (dot(wq[...].reshape(2 * HD, -1), every, 1, 1) * scale).astype(BF16)
    query_other[...] = queries[HD:]
    send_query = begin(
        query_other, query.at[pl.ds(0, HD), pl.ds(256, 256)], sem_ps.at[0], sem_pr.at[0], plane(4)
    )
    keys[0, core] = packed[:, : 2 * HD]
    for distance in range(1, 4):
        begin(
            keys.at[0, core], keys.at[distance, core], sem_zs.at[distance], sem_zr.at[distance], plane(distance)
        )

    def send_sibling(slot):
        block = keys.at[slot, core]
        return remote(block, block, sem_gs.at[slot], sem_cr.at[slot], sibling)

    def from_sibling(slot):
        block = keys.at[slot, 1 - core]
        return remote(block, block, sem_gs.at[slot], sem_cr.at[slot], sibling)

    def from_plane(slot):
        block = keys.at[slot, core]
        return remote(block, block, sem_zs.at[slot], sem_zr.at[slot], plane(4))

    def spread(distance):
        return remote(
            keys.at[4, core], keys.at[4 + distance, core], sem_zs.at[4 + distance], sem_zr.at[4 + distance], plane(distance)
        )

    send_sibling(0).start()
    copies_out = [
        begin(w_out, wo.at[distance, mate], sem_os.at[distance], sem_or.at[distance], chip(distance))
        for distance in range(7, 0, -1)
    ]
    query[0:HD, 0:256] = queries[:HD]
    query[HD:, :] = jnp.zeros((HD, 512), BF16)
    top[...] = jnp.full(top.shape, -1e30, F32)
    accum[...] = jnp.zeros(accum.shape, F32)
    ones_lane = lax.broadcasted_iota(jnp.int32, (256, 2 * HD), 1) < HD
    send_query.wait_recv()

    def fold(index, carry):
        slot = index // 8 * 4 + index % 4
        second = index // 4 % 2
        which = core + second - 2 * core * second

        @pl.when(jnp.logical_and(second == 0, slot >= 1))
        def _():
            from_plane(slot).wait_recv()
            send_sibling(slot).start()

        @pl.when(index == 8)
        def _():
            for distance in range(1, 4):
                spread(distance).start()

        @pl.when(second == 1)
        def _():
            from_sibling(slot).wait_recv()

        block = keys[slot, which]
        scores = dot(block, query[...], 1, 0)
        old = top[...]
        new = jnp.maximum(old, jnp.max(scores, axis=0, keepdims=True))
        probs = jnp.exp2(scores - new).astype(BF16)
        values = jnp.where(ones_lane, jnp.ones_like(block), block)
        accum[...] = accum[...] * jnp.exp2(old - new) + dot(values, probs, 0, 0)
        top[...] = new
        return carry

    lax.fori_loop(0, 16, fold, 0)

    final = (accum[HD:, :] / accum[0:1, :]).astype(BF16)
    attended_other[...] = final[:, 256:]
    returned = begin(
        attended_other, attended.at[0, pl.ds(HD, HD)], sem_ps.at[1], sem_pr.at[1], plane(4)
    )
    attended[0, 0:HD] = final[:, :256]
    copies = []
    for distance in range(7, 0, -1):
        copies.append(
            begin(
                attended.at[0, pl.ds(0, HD)], attended.at[distance, pl.ds(0, HD)],
                sem_as.at[0, distance], sem_ar.at[0, distance], chip(distance),
            )
        )
    weights[2][0].wait()
    weights[2][1].wait_recv()
    forwarded = []
    for copy, distance in zip(copies_out, range(7, 0, -1)):
        copy.wait_recv()
        begin(wo.at[distance, mate], wo.at[distance, mate], sem_fs.at[distance], sem_fr.at[distance], sibling)
        theirs = wo.at[distance, 1 - mate]
        forwarded.append(remote(theirs, theirs, sem_fs.at[distance], sem_fr.at[distance], sibling))
    returned.wait_recv()
    for distance in range(7, 0, -1):
        copies.append(
            begin(
                attended.at[0, pl.ds(HD, HD)], attended.at[distance, pl.ds(HD, HD)],
                sem_as.at[1, distance], sem_ar.at[1, distance], chip(distance),
            )
        )
    for copy in forwarded:
        copy.wait_recv()
    for own, sent in weights[3:]:
        own.wait()
        sent.wait_recv()
    for copy in copies:
        copy.wait_recv()
    attn_sum = dot(attended[...].reshape(16 * HD, 256), wo[...].reshape(16 * HD, -1), 0, 0)
    stream[...] = (rows_in[...].reshape(256, -1).astype(F32) + attn_sum).astype(BF16).reshape(stream.shape)

    units = wdown.shape[0] * wdown.shape[1]

    def piece(slot):
        return remote(
            partial.at[lax.bitwise_xor(me, slot)], summed.at[slot], sem_cs.at[0, slot], sem_cs.at[1, slot], chip(slot)
        )

    def feed(index, carry):
        base = 4 * lax.bitwise_xor(1 - index, me // 4)
        rows = stream[pl.ds(base, 4)].reshape(128, -1).astype(F32)
        normed = norm_rows(rows, gain[1:2, :], bias[1:2, :])
        sums = dot(normed, wgv[...].reshape(2 * units, -1), 1, 1)
        gate, value = sums[:, :units], sums[:, units:]
        hidden = (value * (gate * (lax.erf(gate * (0.5**0.5)) + 1.0) * 0.5)).astype(BF16)
        terms = dot(hidden, wdown[...].reshape(units, -1), 1, 0)
        partial[pl.ds(base, 4)] = terms.astype(BF16).reshape(4, 32, -1)
        for offset in range(3, -1, -1):
            distance = 4 - 4 * index + offset

            @pl.when(distance >= 1)
            def _():
                piece(distance).start()

        return carry

    lax.fori_loop(0, 2, feed, 0)
    total = stream[me].astype(F32) + partial[me].astype(F32)
    for distance in range(1, 8):
        piece(distance).wait_recv()
        total += summed[distance].astype(F32)
    result[...] = total.astype(BF16)

    for copy in started:
        copy.wait_send()
    for distance in range(1, 4):
        spread(distance).wait_send()

    def finish(slot, carry):
        send_sibling(slot).wait_send()

        @pl.when(slot >= 1)
        def _():
            piece(slot).wait_send()

        return carry

    lax.fori_loop(0, 8, finish, 0)


def per_device(latent, ln_gain, ln_bias, w_qkv, w_out, w_gate, w_value, w_down):
    width = latent.shape[-1]
    own_units = w_gate.shape[2]
    vmem, anywhere = pl.BlockSpec(memory_space=pltpu.VMEM), pl.BlockSpec(memory_space=pl.ANY)
    dma = pltpu.SemaphoreType.DMA
    stream = pl.pallas_call(
        block_kernel,
        out_shape=jax.ShapeDtypeStruct((32, width), BF16),
        in_specs=[vmem] * 3 + [anywhere] * 5,
        out_specs=vmem,
        scratch_shapes=[
            pltpu.VMEM((8, 32, width), BF16),
            pltpu.VMEM((8, 32, width), BF16),
            pltpu.VMEM((8, 32, width), BF16),
            pltpu.VMEM((8, 32, width), BF16),
            pltpu.VMEM((8, 32, width), BF16),
            pltpu.VMEM((8, 2, 256, 2 * HD), BF16),
            pltpu.VMEM((256, 2 * HD), BF16),
            pltpu.VMEM((2 * HD, 512), BF16),
            pltpu.VMEM((HD, 256), BF16),
            pltpu.VMEM((2, 2 * HD, width), BF16),
            pltpu.VMEM((2, HD, width), BF16),
            pltpu.VMEM((8, 2, HD, width), BF16),
            pltpu.VMEM((4, own_units, width), BF16),
            pltpu.VMEM((2, own_units, width), BF16),
            pltpu.VMEM((1, 512), F32),
            pltpu.VMEM((2 * HD, 512), F32),
            pltpu.VMEM((8, 2 * HD, 256), BF16),
            pltpu.VMEM((HD, 256), BF16),
            dma((6,)),
            dma((6,)),
            dma((6,)),
            dma((8,)),
            dma((8,)),
            dma((8,)),
            dma((8,)),
            dma((8,)),
            dma((8,)),
            dma((2, 8)),
            dma((2, 8)),
            dma((8,)),
            dma((8,)),
            dma((8,)),
            dma((2, 8)),
            dma((8,)),
            dma((2,)),
            dma((2,)),
        ],
        compiler_params=pltpu.CompilerParams(
            collective_id=0, has_side_effects=True, vmem_limit_bytes=56 * 2**20
        ),
        name="transformer_block",
    )(
        latent.reshape(32, width),
        ln_gain[0],
        ln_bias[0],
        w_qkv[0].transpose(1, 0, 2).reshape(3 * HD, width),
        w_out[0],
        w_gate[0].T,
        w_value[0].T,
        w_down[0],
    )
    return stream.reshape(latent.shape)


def solution(mesh):
    return jax.shard_map(
        per_device,
        mesh=mesh,
        in_specs=(
            P("rows", "cols", None),
            P(),
            P(),
            P(None, "cols", None, None),
            P(None, "cols", None),
            P(None, None, "cols"),
            P(None, None, "cols"),
            P(None, "cols", None),
        ),
        out_specs=P("rows", "cols", None),
        check_vma=False,
    )
```

time: 488 us -> 78.2 us (0.16)
  waiting for transfers between devices: 423 us -> 0 us
  Pallas kernels: 0 us -> 74.9 us
  starting transfers between devices: 14.9 us -> 0 us
  matrix products: 14.3 us -> 0 us
  between operations: 13.4 us -> 0.01 us
  other arithmetic: 9.85 us -> 0 us
  local copies, waits for them, and re-layouts: 10.6 us -> 3.09 us
    reduce_scatter x2 -> x0, waiting for transfers between devices: 174 us -> none  [the longest x1 87.6 us: per_device(): lax.psum_scatter(ffn_terms.astype(jnp.bfloat16), 'cols', scatter_dimensio...]
    all_gather x2 -> x0, waiting for transfers between devices: 131 us -> none  [the longest x1 67.1 us: per_device(): lax.all_gather(normed, 'cols', axis=1, tiled=True)]
    ppermute x3 -> x0, waiting for transfers between devices: 118 us -> none  [partner(): return lax.ppermute(block, axis, route)]
    pallas_call x0 -> x1, Pallas kernels: none -> 74.9 us  [per_device(): pl.pallas_call(block_kernel, out_shape=jax.ShapeDtypeStruct((32, width),...]
    ppermute x3 -> x0, starting transfers between devices: 14.8 us -> none  [partner(): return lax.ppermute(block, axis, route)]
    dot_general x13 -> x0, matrix products: 14.3 us -> none  [the longest x4 5.56 us: fold_keys(): jnp.einsum('hqk,khd->hqd', weights.astype(jnp.bfloat16), value_rows, pref...]
    reduce_sum x8 -> x0, other arithmetic: 4.88 us -> none  [the longest x2 2.05 us: norm_rows(): row_mean = jnp.mean(values, axis=-1, keepdims=True)]
  transfers between devices with their start and end apart: 7 -> 0, of which waited for: 7 -> 0; matrix products, arithmetic and copies ran while one was open for 0% -> 0% of each run, Pallas kernels for 0% -> 0%
where the time goes in v2:
time: 78.2 us; the launch traced here: 78 us
  Pallas kernels  74.9 us (96%)
  local copies, waits for them, and re-layouts  3.09 us (4%)
    pallas_call x1, Pallas kernels, per_device(): pl.pallas_call(block_kernel, out_shape=jax.ShapeDtypeStruct((32, width),...  74.9 us

profile of v2, /device:TPU:1, one launch (start us, length us, event | category | flops | bytes accessed | tf_op | source)
XLA Modules:
  0.0 78.0 jit_solution(361773983186221798)
XLA Ops:
  0.0 1.5 %reshape.9.latent = bf16[32,1280]{1,0:T(8,128)(2,1)} reshape(bf16[8,4,1280]{2,1,0:T(4,128)(2,1)} %param.8) | data formatting | bytes 163840 | tf_op jit(solution)/shard_map/reshape | solution.py:322
  1.5 74.9 %transformer_block.1 = bf16[32,1280]{1,0:T(8,128)(2,1)} custom-call(bf16[32,1280]{1,0:T(8,128)(2,1)} %reshape.9.latent, f32[2,1280]{1,0:T(2,128)} %bitcast.20, f32[2,1280]{1,0:T(2,128)} %bitcast.21, bf16[192,1280]{1,0:T(8,128)(2,1)} %bitcast.18, bf16[64,1280]{1,0:T(8,128)(2,1)} %bitcast.19, bf16[320,1280]{1,0:T(8,128)(2,1)} %bitcast.15, ...), custom_call_target="tpu_custom_call" | custom-call | tf_op jit(solution)/shard_map/transformer_block/pallas_call | solution.py:274
  76.4 1.5 %reshape.11 = bf16[8,4,1280]{2,1,0:T(4,128)(2,1)} reshape(bf16[32,1280]{1,0:T(8,128)(2,1)} %transformer_block.1) | data formatting | bytes 163840 | tf_op jit(solution)/shard_map/reshape | solution.py:331

commit v3 on v2

v3 whole, which is shorter than its diff:
```python
import math

import jax
import jax.numpy as jnp
from jax import lax
from jax.experimental import pallas as pl
from jax.experimental.pallas import tpu as pltpu
from jax.sharding import PartitionSpec as P

HD = 64
MESH = pl.DeviceIdType.MESH
F32, BF16 = jnp.float32, jnp.bfloat16


def norm_rows(values, gain, bias):
    row_mean = jnp.mean(values, axis=-1, keepdims=True)
    centred = values - row_mean
    row_var = jnp.mean(centred * centred, axis=-1, keepdims=True)
    return (centred * lax.rsqrt(row_var + 1e-05) * gain + bias).astype(BF16)


def dot(left, right, left_dim, right_dim):
    return lax.dot_general(
        left, right, (((left_dim,), (right_dim,)), ((), ())), preferred_element_type=F32
    )


def block_kernel(
    latent, gain_in, bias_in, w_qkv, w_out, w_gate, w_value, w_down, result,
    rows_in, rows_far, gain, bias, tokens, stream, partial, summed, keys, query,
    wkv, wq, wo, wgv, wdown, top, accum, attended, attended_other,
    sem_l, sem_w, sem_ws, sem_wr, sem_os, sem_or, sem_fs, sem_fr, sem_xs, sem_xr, sem_ys, sem_yr,
    sem_as, sem_ar, sem_zs, sem_zr, sem_gs, sem_gr, sem_cs, sem_cr, sem_ps, sem_pr,
):
    row, col = lax.axis_index("rows"), lax.axis_index("cols")
    core, me = col % 2, col // 2
    mate = lax.bitwise_xor(core, row % 8 // 4)
    sibling = (row, col + 1 - 2 * core)
    width = gain.shape[1]

    def chip(distance):
        return (row, lax.bitwise_xor(col, 2 * distance))

    def plane(distance):
        return (lax.bitwise_xor(row, distance), col)

    def remote(src, dst, send, recv, device):
        return pltpu.make_async_remote_copy(
            src_ref=src, dst_ref=dst, send_sem=send, recv_sem=recv, device_id=device, device_id_type=MESH
        )

    started = []

    def begin(*args):
        copy = remote(*args)
        copy.start()
        started.append(copy)
        return copy

    barrier = pltpu.get_barrier_semaphore()
    pl.semaphore_signal(barrier, inc=1, device_id=plane(4), device_id_type=MESH)
    for distance in range(7, 0, -1):
        pl.semaphore_signal(barrier, inc=1, device_id=chip(distance), device_id_type=MESH)
    for distance in range(1, 4):
        pl.semaphore_signal(barrier, inc=1, device_id=plane(distance), device_id_type=MESH)
    pl.semaphore_signal(barrier, inc=1, device_id=sibling, device_id_type=MESH)

    local = []

    def begin_local(src, dst, sem):
        copy = pltpu.make_async_copy(src, dst, sem)
        copy.start()
        return copy

    local = [
        begin_local(latent, rows_in.at[me], sem_l.at[0]),
        begin_local(gain_in, gain, sem_l.at[1]),
        begin_local(bias_in, bias, sem_l.at[2]),
    ]
    homes = [
        (w_qkv.at[pl.ds(HD, 2 * HD)], wkv.at[mate], wkv.at[mate]),
        (w_qkv.at[pl.ds(0, HD)], wq.at[mate], wq.at[mate]),
        (w_out, wo.at[0, mate], wo.at[0, mate]),
        (w_gate, wgv.at[0], wgv.at[1]),
        (w_value, wgv.at[2], wgv.at[3]),
        (w_down, wdown.at[0], wdown.at[1]),
    ]
    own_weights = [begin_local(src, mine, sem_w.at[index]) for index, (src, mine, _) in enumerate(homes)]
    pl.semaphore_wait(barrier, 12)

    across = begin(latent, rows_far.at[me], sem_ps.at[0], sem_pr.at[0], plane(4))
    for distance in range(7, 0, -1):
        begin(latent, rows_in.at[me], sem_xs.at[distance], sem_xr.at[distance], chip(distance))
    sent_weights = [
        begin(src, theirs, sem_ws.at[index], sem_wr.at[index], sibling)
        for index, (src, _, theirs) in enumerate(homes)
    ]

    def near_copy(distance):
        block = rows_in.at[lax.bitwise_xor(me, distance)]
        return remote(block, block, sem_xs.at[distance], sem_xr.at[distance], chip(distance))

    def far_copy(distance):
        block = rows_far.at[lax.bitwise_xor(me, distance)]
        return remote(block, block, sem_ys.at[distance], sem_yr.at[distance], chip(distance))

    def near_norm(distance):
        slot = lax.bitwise_xor(me, distance)
        rows = rows_in[slot].astype(F32).reshape(32, width)
        stream[slot] = rows.astype(BF16)
        tokens[0, slot] = norm_rows(rows, gain[0:1, :], bias[0:1, :])

    def near_step(distance, carry):
        near_copy(distance).wait_recv()
        near_norm(distance)
        return carry

    for copy in local:
        copy.wait()
    near_norm(0)
    across.wait_recv()
    for distance in range(7, 0, -1):
        begin(rows_far.at[me], rows_far.at[me], sem_ys.at[distance], sem_yr.at[distance], chip(distance))
    lax.fori_loop(1, 8, near_step, 0)
    for index in range(2):
        own_weights[index].wait()
        sent_weights[index].wait_recv()

    scale = HD ** (-0.5) * math.log2(math.e)

    def project(which, slot, part):
        piece = tokens[which, pl.ds(4 * part, 4)].reshape(128, width)
        place = pl.ds(pl.multiple_of(128 * part, 128), 128)
        keys[slot, core, place] = dot(piece, wkv[0], 1, 1).astype(BF16)
        query[which, 0:HD, place] = (dot(wq[0], piece, 1, 1) * scale).astype(BF16)

    def send_sibling(slot):
        block = keys.at[slot, core]
        return remote(block, block, sem_gs.at[slot], sem_gr.at[slot], sibling)

    def from_sibling(slot):
        block = keys.at[slot, 1 - core]
        return remote(block, block, sem_gs.at[slot], sem_gr.at[slot], sibling)

    def from_plane(slot, part):
        block = keys.at[slot, core, pl.ds(128 * part, 128)]
        return remote(block, block, sem_zs.at[slot, part], sem_zr.at[slot, part], plane(4))

    for part in range(2):
        project(0, 0, part)
    for distance in range(3, 0, -1):
        begin(
            keys.at[0, core], keys.at[distance, core],
            sem_zs.at[distance, 0], sem_zr.at[distance, 0], plane(distance),
        )
    send_sibling(0).start()
    query[:, HD:, :] = jnp.zeros((2, HD, 256), BF16)
    top[...] = jnp.full(top.shape, -1e30, F32)
    accum[...] = jnp.zeros(accum.shape, F32)
    ones_lane = lax.broadcasted_iota(jnp.int32, (512, 2 * HD), 1) < HD

    def fold(slot, which):
        block = keys[slot].reshape(512, 2 * HD)
        scores = dot(block, query[which], 1, 0)
        old = top[which]
        new = jnp.maximum(old, jnp.max(scores, axis=0, keepdims=True))
        probs = jnp.exp2(scores - new).astype(BF16)
        values = jnp.where(ones_lane, jnp.ones_like(block), block)
        accum[which] = accum[which] * jnp.exp2(old - new) + dot(values, probs, 0, 0)
        top[which] = new

    def attended_by(which):
        return (accum[which, HD:, :] / accum[which, 0:1, :]).astype(BF16)

    from_sibling(0).wait_recv()
    fold(0, 0)

    def far_step(distance, carry):
        @pl.when(distance >= 1)
        def _():
            far_copy(distance).wait_recv()

        slot = lax.bitwise_xor(me, distance)
        rows = rows_far[slot].astype(F32).reshape(32, width)
        tokens[1, slot] = norm_rows(rows, gain[0:1, :], bias[0:1, :])
        return carry

    for turn in range(2):
        part = lax.bitwise_xor(me // 4, turn)
        lax.fori_loop(4 * turn, 4 * turn + 4, far_step, 0)
        project(1, 4, part)
        place = pl.ds(pl.multiple_of(128 * part, 128), 128)
        for distance in range(3, 0, -1):
            begin(
                keys.at[4, core, place], keys.at[4 + distance, core, place],
                sem_zs.at[4 + distance, turn], sem_zr.at[4 + distance, turn], plane(distance),
            )
    send_sibling(4).start()
    copies_out = [
        begin(w_out, wo.at[distance, mate], sem_os.at[distance], sem_or.at[distance], chip(distance))
        for distance in range(7, 0, -1)
    ]

    def early(index, carry):
        slots, halves = carry
        slot, which = slots % 8, halves % 2

        @pl.when(index == 1)
        def _():
            for near in range(1, 4):
                block = keys.at[near, core]
                remote(block, block, sem_zs.at[near, 0], sem_zr.at[near, 0], plane(near)).wait_recv()
                send_sibling(near).start()

        @pl.when(jnp.logical_or(index == 1, jnp.logical_and(index >= 3, index < 6)))
        def _():
            from_sibling(slot).wait_recv()

        @pl.when(index == 6)
        def _():
            for far in range(5, 8):
                from_plane(far, 0).wait_recv()
                from_plane(far, 1).wait_recv()
                send_sibling(far).start()

        fold(slot, which)
        return (slots // 8, halves // 2)

    order = sum(slot * 8**place for place, slot in enumerate((0, 4, 4, 1, 2, 3, 1, 2, 3)))
    halves = sum(half * 2**place for place, half in enumerate((1, 1, 0, 1, 1, 1, 0, 0, 0)))
    lax.fori_loop(0, 9, early, (jnp.int32(order), jnp.int32(halves)))

    returned = remote(
        attended_other, attended.at[0, pl.ds(HD, HD)], sem_ps.at[1], sem_pr.at[1], plane(4)
    )

    def late(index, carry):
        slot, which = 5 + index % 3, 1 - index // 3

        @pl.when(index < 3)
        def _():
            from_sibling(slot).wait_recv()

        @pl.when(index == 3)
        def _():
            attended_other[...] = attended_by(1)
            returned.start()

        fold(slot, which)
        return carry

    lax.fori_loop(0, 6, late, 0)

    attended[0, 0:HD] = attended_by(0)
    copies = []
    for distance in range(7, 0, -1):
        copies.append(
            begin(
                attended.at[0, pl.ds(0, HD)], attended.at[distance, pl.ds(0, HD)],
                sem_as.at[0, distance], sem_ar.at[0, distance], chip(distance),
            )
        )
    for index in range(2, 6):
        own_weights[index].wait()
        sent_weights[index].wait_recv()
    returned.wait_recv()
    for distance in range(7, 0, -1):
        copies.append(
            begin(
                attended.at[0, pl.ds(HD, HD)], attended.at[distance, pl.ds(HD, HD)],
                sem_as.at[1, distance], sem_ar.at[1, distance], chip(distance),
            )
        )
    forwarded = []
    for copy, distance in zip(copies_out, range(7, 0, -1)):
        copy.wait_recv()
        begin(wo.at[distance, mate], wo.at[distance, mate], sem_fs.at[distance], sem_fr.at[distance], sibling)
        theirs = wo.at[distance, 1 - mate]
        forwarded.append(remote(theirs, theirs, sem_fs.at[distance], sem_fr.at[distance], sibling))
    for copy in forwarded:
        copy.wait_recv()
    for copy in copies:
        copy.wait_recv()
    attn_sum = dot(attended[...].reshape(16 * HD, 256), wo[...].reshape(16 * HD, width), 0, 0)
    stream[...] = (stream[...].reshape(256, width).astype(F32) + attn_sum).astype(BF16).reshape(stream.shape)

    units = wdown.shape[0] * wdown.shape[1]

    def piece(slot):
        return remote(
            partial.at[lax.bitwise_xor(me, slot)], summed.at[slot], sem_cs.at[slot], sem_cr.at[slot], chip(slot)
        )

    def feed(index, carry):
        base = 4 * lax.bitwise_xor(1 - index, me // 4)
        rows = stream[pl.ds(base, 4)].reshape(128, width).astype(F32)
        normed = norm_rows(rows, gain[1:2, :], bias[1:2, :])
        sums = dot(normed, wgv[...].reshape(2 * units, width), 1, 1)
        gate, value = sums[:, :units], sums[:, units:]
        hidden = (value * (gate * (lax.erf(gate * (0.5**0.5)) + 1.0) * 0.5)).astype(BF16)
        terms = dot(hidden, wdown[...].reshape(units, width), 1, 0)
        partial[pl.ds(base, 4)] = terms.astype(BF16).reshape(4, 32, width)
        for offset in range(3, -1, -1):
            distance = 4 - 4 * index + offset

            @pl.when(distance >= 1)
            def _():
                piece(distance).start()

        return carry

    lax.fori_loop(0, 2, feed, 0)
    total = stream[me].astype(F32) + partial[me].astype(F32)
    for distance in range(1, 8):
        piece(distance).wait_recv()
        total += summed[distance].astype(F32)
    result[...] = total.reshape(8, 4, width).astype(BF16)

    for copy in started:
        copy.wait_send()
    returned.wait_send()

    def finish(slot, carry):
        send_sibling(slot).wait_send()

        @pl.when(slot >= 1)
        def _():
            piece(slot).wait_send()

        return carry

    lax.fori_loop(0, 8, finish, 0)


def per_device(latent, ln_gain, ln_bias, w_qkv, w_out, w_gate, w_value, w_down):
    width = latent.shape[-1]
    own_units = w_gate.shape[2]
    vmem, anywhere = pl.BlockSpec(memory_space=pltpu.VMEM), pl.BlockSpec(memory_space=pl.ANY)
    dma = pltpu.SemaphoreType.DMA
    return pl.pallas_call(
        block_kernel,
        out_shape=jax.ShapeDtypeStruct(latent.shape, BF16),
        in_specs=[anywhere] * 8,
        out_specs=vmem,
        scratch_shapes=[
            pltpu.VMEM((8, *latent.shape), BF16),
            pltpu.VMEM((8, *latent.shape), BF16),
            pltpu.VMEM((2, width), F32),
            pltpu.VMEM((2, width), F32),
            pltpu.VMEM((2, 8, 32, width), BF16),
            pltpu.VMEM((8, 32, width), BF16),
            pltpu.VMEM((8, 32, width), BF16),
            pltpu.VMEM((8, 32, width), BF16),
            pltpu.VMEM((8, 2, 256, 2 * HD), BF16),
            pltpu.VMEM((2, 2 * HD, 256), BF16),
            pltpu.VMEM((2, 2 * HD, width), BF16),
            pltpu.VMEM((2, HD, width), BF16),
            pltpu.VMEM((8, 2, HD, width), BF16),
            pltpu.VMEM((4, own_units, width), BF16),
            pltpu.VMEM((2, own_units, width), BF16),
            pltpu.VMEM((2, 1, 256), F32),
            pltpu.VMEM((2, 2 * HD, 256), F32),
            pltpu.VMEM((8, 2 * HD, 256), BF16),
            pltpu.VMEM((HD, 256), BF16),
            dma((3,)),
            dma((6,)),
            dma((6,)),
            dma((6,)),
            dma((8,)),
            dma((8,)),
            dma((8,)),
            dma((8,)),
            dma((8,)),
            dma((8,)),
            dma((8,)),
            dma((8,)),
            dma((2, 8)),
            dma((2, 8)),
            dma((8, 2)),
            dma((8, 2)),
            dma((8,)),
            dma((8,)),
            dma((8,)),
            dma((8,)),
            dma((2,)),
            dma((2,)),
        ],
        compiler_params=pltpu.CompilerParams(
            collective_id=0, has_side_effects=True, vmem_limit_bytes=56 * 2**20
        ),
        name="transformer_block",
    )(
        latent,
        ln_gain[0],
        ln_bias[0],
        w_qkv[0].transpose(1, 0, 2).reshape(3 * HD, width),
        w_out[0],
        w_gate[0].T,
        w_value[0].T,
        w_down[0],
    )


def solution(mesh):
    return jax.shard_map(
        per_device,
        mesh=mesh,
        in_specs=(
            P("rows", "cols", None),
            P(),
            P(),
            P(None, "cols", None, None),
            P(None, "cols", None),
            P(None, None, "cols"),
            P(None, None, "cols"),
            P(None, "cols", None),
        ),
        out_specs=P("rows", "cols", None),
        check_vma=False,
    )
```

time: 78.2 us -> 74.1 us (0.948)
  Pallas kernels: 74.9 us -> 72.4 us
  local copies, waits for them, and re-layouts: 3.09 us -> 1.55 us
    reshape x2 -> x0, local copies, waits for them, and re-layouts: 3.09 us -> none  [the longest x1 1.55 us: per_device(): return stream.reshape(latent.shape)]
    pallas_call x1, Pallas kernels: 74.9 us -> 72.4 us  [per_device(): pl.pallas_call(block_kernel, out_shape=jax.ShapeDtypeStruct(latent.shape,...]
    unnamed x0 -> x1, local copies, waits for them, and re-layouts: none -> 1.55 us
where the time goes in v3:
time: 74.1 us; the launch traced here: 74 us
  Pallas kernels  72.4 us (98%)
  local copies, waits for them, and re-layouts  1.55 us (2%)
    pallas_call x1, Pallas kernels, per_device(): pl.pallas_call(block_kernel, out_shape=jax.ShapeDtypeStruct(latent.shape,...  72.4 us
    unnamed x1, local copies, waits for them, and re-layouts  1.55 us

profile of v3, /device:TPU:1, one launch (start us, length us, event | category | flops | bytes accessed | tf_op | source)
XLA Modules:
  0.0 74.0 jit_solution(4493149466996330315)
XLA Ops:
  0.0 72.4 %transformer_block.1 = bf16[8,4,1280]{2,1,0:T(4,128)(2,1)} custom-call(bf16[8,4,1280]{2,1,0:T(4,128)(2,1)} %latent.1, f32[2,1280]{1,0:T(2,128)} %bitcast.20, f32[2,1280]{1,0:T(2,128)} %bitcast.21, bf16[192,1280]{1,0:T(8,128)(2,1)} %bitcast.18, bf16[64,1280]{1,0:T(8,128)(2,1)} %bitcast.19, bf16[320,1280]{1,0:T(8,128)(2,1)} %bitcast.15, ...), custom_call_target="tpu_custom_call" | custom-call | tf_op jit(solution)/shard_map/transformer_block/pallas_call | solution.py:340
  72.4 1.6 %copy.10 = bf16[8,4,1280]{2,1,0:T(4,128)(2,1)} copy(bf16[8,4,1280]{2,1,0:T(4,128)(2,1)} %transformer_block.1) | data formatting | bytes 163840

commit v4 on v3

v4 whole, which is shorter than its diff:
```python
import math

import jax
import jax.numpy as jnp
from jax import lax
from jax.experimental import pallas as pl
from jax.experimental.pallas import tpu as pltpu
from jax.sharding import PartitionSpec as P

HD = 64
MESH = pl.DeviceIdType.MESH
F32, BF16 = jnp.float32, jnp.bfloat16


def norm_rows(values, gain, bias):
    row_mean = jnp.mean(values, axis=-1, keepdims=True)
    centred = values - row_mean
    row_var = jnp.mean(centred * centred, axis=-1, keepdims=True)
    return (centred * lax.rsqrt(row_var + 1e-05) * gain + bias).astype(BF16)


def dot(left, right, left_dim, right_dim):
    return lax.dot_general(
        left, right, (((left_dim,), (right_dim,)), ((), ())), preferred_element_type=F32
    )


def block_kernel(
    latent, gain_in, bias_in, w_qkv, w_out, w_gate, w_value, w_down, result,
    rows_in, rows_far, gain, bias, tokens, stream, partial, summed, keys, query,
    wkv, wq, wo, wgv, wgv_t, wdown, top, accum, attn_sum, attended, attended_other,
    sem_l, sem_w, sem_ws, sem_wr, sem_os, sem_or, sem_fs, sem_fr, sem_xs, sem_xr, sem_ys, sem_yr,
    sem_as, sem_ar, sem_zs, sem_zr, sem_gs, sem_gr, sem_cs, sem_cr, sem_ps, sem_pr,
):
    row, col = lax.axis_index("rows"), lax.axis_index("cols")
    core, me = col % 2, col // 2
    mate = lax.bitwise_xor(core, row % 8 // 4)
    sibling = (row, col + 1 - 2 * core)
    width = gain.shape[1]

    def chip(distance):
        return (row, lax.bitwise_xor(col, 2 * distance))

    def plane(distance):
        return (lax.bitwise_xor(row, distance), col)

    def remote(src, dst, send, recv, device):
        return pltpu.make_async_remote_copy(
            src_ref=src, dst_ref=dst, send_sem=send, recv_sem=recv, device_id=device, device_id_type=MESH
        )

    started = []

    def begin(*args):
        copy = remote(*args)
        copy.start()
        started.append(copy)
        return copy

    barrier = pltpu.get_barrier_semaphore()
    pl.semaphore_signal(barrier, inc=1, device_id=plane(4), device_id_type=MESH)
    for distance in range(7, 0, -1):
        pl.semaphore_signal(barrier, inc=1, device_id=chip(distance), device_id_type=MESH)
    for distance in range(1, 4):
        pl.semaphore_signal(barrier, inc=1, device_id=plane(distance), device_id_type=MESH)
    pl.semaphore_signal(barrier, inc=1, device_id=sibling, device_id_type=MESH)

    local = []

    def begin_local(src, dst, sem):
        copy = pltpu.make_async_copy(src, dst, sem)
        copy.start()
        return copy

    local = [
        begin_local(latent, rows_in.at[me], sem_l.at[0]),
        begin_local(gain_in, gain, sem_l.at[1]),
        begin_local(bias_in, bias, sem_l.at[2]),
    ]
    homes = [
        (w_qkv.at[pl.ds(HD, 2 * HD)], wkv.at[mate], wkv.at[mate]),
        (w_qkv.at[pl.ds(0, HD)], wq.at[mate], wq.at[mate]),
        (w_out, wo.at[0, mate], wo.at[0, mate]),
        (w_gate, wgv.at[0], wgv.at[1]),
        (w_value, wgv.at[2], wgv.at[3]),
        (w_down, wdown.at[0], wdown.at[1]),
    ]

    def fetch(first, last):
        return [begin_local(homes[index][0], homes[index][1], sem_w.at[index]) for index in range(first, last)]

    def share(first, last):
        return [
            begin(homes[index][0], homes[index][2], sem_ws.at[index], sem_wr.at[index], sibling)
            for index in range(first, last)
        ]

    own_weights = fetch(0, 3)
    pl.semaphore_wait(barrier, 12)

    across = [
        begin(latent.at[pl.ds(4 * part, 4)], rows_far.at[me, part], sem_ps.at[part], sem_pr.at[part], plane(4))
        for part in range(2)
    ]
    for distance in range(7, 0, -1):
        begin(latent, rows_in.at[me], sem_xs.at[distance], sem_xr.at[distance], chip(distance))
    sent_weights = share(0, 3)

    def spread_out(part, first, count):
        return [
            begin(
                w_out.at[pl.ds(first, count)], wo.at[distance, mate, pl.ds(first, count)],
                sem_os.at[part, distance], sem_or.at[part, distance], chip(distance),
            )
            for distance in range(7, 0, -1)
        ]

    copies_out = spread_out(0, 0, 16)

    def near_copy(distance):
        block = rows_in.at[lax.bitwise_xor(me, distance)]
        return remote(block, block, sem_xs.at[distance], sem_xr.at[distance], chip(distance))

    def far_copy(part, distance):
        block = rows_far.at[lax.bitwise_xor(me, distance), part]
        return remote(block, block, sem_ys.at[part, distance], sem_yr.at[part, distance], chip(distance))

    def near_norm(distance):
        slot = lax.bitwise_xor(me, distance)
        for part in range(2):
            rows = rows_in[slot, pl.ds(4 * part, 4)].astype(F32).reshape(16, width)
            stream[part, slot] = rows.astype(BF16)
            tokens[0, part, slot] = norm_rows(rows, gain[0:1, :], bias[0:1, :])

    def near_step(distance, carry):
        near_copy(distance).wait_recv()
        near_norm(distance)
        return carry

    for copy in local:
        copy.wait()
    near_norm(0)
    for part in range(2):
        across[part].wait_recv()
        for distance in range(7, 0, -1):
            mine = rows_far.at[me, part]
            begin(mine, mine, sem_ys.at[part, distance], sem_yr.at[part, distance], chip(distance))
    own_weights += fetch(3, 6)
    sent_weights += share(3, 6)
    lax.fori_loop(1, 8, near_step, 0)
    for index in range(2):
        own_weights[index].wait()
        sent_weights[index].wait_recv()

    scale = HD ** (-0.5) * math.log2(math.e)

    def project(which, part):
        piece = tokens[which, part].reshape(128, width)
        place = pl.ds(128 * part, 128)
        keys[4 * which, core, place] = dot(piece, wkv[0], 1, 1).astype(BF16)
        query[0:HD, pl.ds(256 * which + 128 * part, 128)] = (dot(wq[0], piece, 1, 1) * scale).astype(BF16)

    def send_sibling(slot):
        block = keys.at[slot, core]
        return remote(block, block, sem_gs.at[slot], sem_gr.at[slot], sibling)

    def from_sibling(slot):
        block = keys.at[slot, 1 - core]
        return remote(block, block, sem_gs.at[slot], sem_gr.at[slot], sibling)

    def from_plane(slot, part):
        block = keys.at[slot, core, pl.ds(128 * part, 128)]
        return remote(block, block, sem_zs.at[slot, part], sem_zr.at[slot, part], plane(4))

    for part in range(2):
        project(0, part)
    for distance in range(3, 0, -1):
        begin(
            keys.at[0, core], keys.at[distance, core],
            sem_zs.at[distance, 0], sem_zr.at[distance, 0], plane(distance),
        )
    send_sibling(0).start()
    query[HD:, :] = jnp.zeros((HD, 512), BF16)
    own_weights[3].wait()
    own_weights[4].wait()
    sent_weights[3].wait_recv()
    sent_weights[4].wait_recv()
    for index in range(4):
        wgv_t[:, pl.ds(320 * index, 320)] = wgv[index].T

    def far_step(distance, part):
        @pl.when(distance >= 1)
        def _():
            far_copy(part, distance).wait_recv()

        slot = lax.bitwise_xor(me, distance)
        rows = rows_far[slot, part].astype(F32).reshape(16, width)
        tokens[1, part, slot] = norm_rows(rows, gain[0:1, :], bias[0:1, :])
        return part

    for part in range(2):
        lax.fori_loop(0, 8, far_step, part)
        project(1, part)
        place = pl.ds(128 * part, 128)
        for distance in range(3, 0, -1):
            begin(
                keys.at[4, core, place], keys.at[4 + distance, core, place],
                sem_zs.at[4 + distance, part], sem_zr.at[4 + distance, part], plane(distance),
            )
    send_sibling(4).start()
    copies_out += spread_out(1, 16, 48)

    def scored(block, first, count):
        return dot(block, query[:, first : first + count], 1, 0)

    def summed_values(block, probs):
        lanes = lax.broadcasted_iota(jnp.int32, block.shape, 1)
        return dot(jnp.where(lanes < HD, jnp.ones_like(block), block), probs, 0, 0)

    def fold(block, first, count):
        scores = scored(block, first, count)
        old = top[:, first : first + count]
        new = jnp.maximum(old, jnp.max(scores, axis=0, keepdims=True))
        probs = jnp.exp2(scores - new).astype(BF16)
        accum[:, first : first + count] = accum[:, first : first + count] * jnp.exp2(old - new) + summed_values(block, probs)
        top[:, first : first + count] = new

    def attended_by(first):
        return (accum[HD:, first : first + 256] / accum[0:1, first : first + 256]).astype(BF16)

    for near in range(1, 4):
        block = keys.at[near, core]
        remote(block, block, sem_zs.at[near, 0], sem_zr.at[near, 0], plane(near)).wait_recv()
        send_sibling(near).start()
    for near in range(4):
        from_sibling(near).wait_recv()
    block = keys[0:4].reshape(2048, 2 * HD)
    scores = scored(block, 0, 512)
    first_top = jnp.max(scores, axis=0, keepdims=True)
    top[...] = first_top
    accum[...] = summed_values(block, jnp.exp2(scores - first_top).astype(BF16))
    for far in range(5, 8):
        from_plane(far, 0).wait_recv()
        from_plane(far, 1).wait_recv()
        send_sibling(far).start()
    fold(keys[pl.ds(4, 4), core].reshape(1024, 2 * HD), 256, 256)
    for far in range(4, 8):
        from_sibling(far).wait_recv()
    fold(keys[pl.ds(4, 4), 1 - core].reshape(1024, 2 * HD), 256, 256)
    attended_other[...] = attended_by(256)
    returned = begin(
        attended_other, attended.at[0, pl.ds(HD, HD)], sem_ps.at[2], sem_pr.at[2], plane(4)
    )
    fold(keys[4:8].reshape(2048, 2 * HD), 0, 256)

    attended[0, 0:HD] = attended_by(0)
    copies = []
    for distance in range(7, 0, -1):
        copies.append(
            begin(
                attended.at[0, pl.ds(0, HD)], attended.at[distance, pl.ds(0, HD)],
                sem_as.at[0, distance], sem_ar.at[0, distance], chip(distance),
            )
        )
    returned.wait_recv()
    for distance in range(7, 0, -1):
        copies.append(
            begin(
                attended.at[0, pl.ds(HD, HD)], attended.at[distance, pl.ds(HD, HD)],
                sem_as.at[1, distance], sem_ar.at[1, distance], chip(distance),
            )
        )
    own_weights[2].wait()
    sent_weights[2].wait_recv()
    forwarded = []
    for index, distance in enumerate(range(7, 0, -1)):
        copies_out[index].wait_recv()
        copies_out[7 + index].wait_recv()
        begin(wo.at[distance, mate], wo.at[distance, mate], sem_fs.at[distance], sem_fr.at[distance], sibling)
        theirs = wo.at[distance, 1 - mate]
        forwarded.append(remote(theirs, theirs, sem_fs.at[distance], sem_fr.at[distance], sibling))
    for copy in forwarded + copies[:7]:
        copy.wait_recv()

    def projected(part):
        heads = attended[:, HD * part : HD * (part + 1)].reshape(8 * HD, 256)
        return dot(heads, wo[:, part].reshape(8 * HD, width), 0, 0)

    attn_sum[...] = projected(0)
    own_weights[5].wait()
    sent_weights[5].wait_recv()
    for copy in copies[7:]:
        copy.wait_recv()
    total = stream[...].reshape(256, width).astype(F32) + (attn_sum[...] + projected(1))
    stream[...] = total.astype(BF16).reshape(stream.shape)

    units = wdown.shape[0] * wdown.shape[1]

    def piece(slot):
        return remote(
            partial.at[:, lax.bitwise_xor(me, slot)], summed.at[slot], sem_cs.at[slot], sem_cr.at[slot], chip(slot)
        )

    def feed(index, carry):
        base = 4 * lax.bitwise_xor(1 - index, me // 4)
        rows = stream[:, pl.ds(base, 4)].reshape(128, width).astype(F32)
        normed = norm_rows(rows, gain[1:2, :], bias[1:2, :])
        sums = dot(normed, wgv_t[...], 1, 0)
        gate, value = sums[:, :units], sums[:, units:]
        hidden = (value * (gate * (lax.erf(gate * (0.5**0.5)) + 1.0) * 0.5)).astype(BF16)
        terms = dot(hidden, wdown[...].reshape(units, width), 1, 0)
        partial[:, pl.ds(base, 4)] = terms.astype(BF16).reshape(2, 4, 16, width)
        for offset in range(3, -1, -1):
            distance = 4 - 4 * index + offset

            @pl.when(distance >= 1)
            def _():
                piece(distance).start()

        return carry

    lax.fori_loop(0, 2, feed, 0)
    total = stream[:, me].astype(F32) + partial[:, me].astype(F32)
    for distance in range(1, 8):
        piece(distance).wait_recv()
        total += summed[distance].astype(F32)
    result[...] = total.reshape(8, 4, width).astype(BF16)

    for copy in started:
        copy.wait_send()

    def finish(slot, carry):
        send_sibling(slot).wait_send()

        @pl.when(slot >= 1)
        def _():
            piece(slot).wait_send()

        return carry

    lax.fori_loop(0, 8, finish, 0)


def per_device(latent, ln_gain, ln_bias, w_qkv, w_out, w_gate, w_value, w_down):
    width = latent.shape[-1]
    own_units = w_gate.shape[2]
    vmem, anywhere = pl.BlockSpec(memory_space=pltpu.VMEM), pl.BlockSpec(memory_space=pl.ANY)
    dma = pltpu.SemaphoreType.DMA
    return pl.pallas_call(
        block_kernel,
        out_shape=jax.ShapeDtypeStruct(latent.shape, BF16),
        in_specs=[anywhere] * 8,
        out_specs=vmem,
        scratch_shapes=[
            pltpu.VMEM((8, *latent.shape), BF16),
            pltpu.VMEM((8, 2, 4, *latent.shape[1:]), BF16),
            pltpu.VMEM((2, width), F32),
            pltpu.VMEM((2, width), F32),
            pltpu.VMEM((2, 2, 8, 16, width), BF16),
            pltpu.VMEM((2, 8, 16, width), BF16),
            pltpu.VMEM((2, 8, 16, width), BF16),
            pltpu.VMEM((8, 2, 16, width), BF16),
            pltpu.VMEM((8, 2, 256, 2 * HD), BF16),
            pltpu.VMEM((2 * HD, 512), BF16),
            pltpu.VMEM((2, 2 * HD, width), BF16),
            pltpu.VMEM((2, HD, width), BF16),
            pltpu.VMEM((8, 2, HD, width), BF16),
            pltpu.VMEM((4, own_units, width), BF16),
            pltpu.VMEM((width, 4 * own_units), BF16),
            pltpu.VMEM((2, own_units, width), BF16),
            pltpu.VMEM((1, 512), F32),
            pltpu.VMEM((2 * HD, 512), F32),
            pltpu.VMEM((256, width), F32),
            pltpu.VMEM((8, 2 * HD, 256), BF16),
            pltpu.VMEM((HD, 256), BF16),
            dma((3,)),
            dma((6,)),
            dma((6,)),
            dma((6,)),
            dma((2, 8)),
            dma((2, 8)),
            dma((8,)),
            dma((8,)),
            dma((8,)),
            dma((8,)),
            dma((2, 8)),
            dma((2, 8)),
            dma((2, 8)),
            dma((2, 8)),
            dma((8, 2)),
            dma((8, 2)),
            dma((8,)),
            dma((8,)),
            dma((8,)),
            dma((8,)),
            dma((3,)),
            dma((3,)),
        ],
        compiler_params=pltpu.CompilerParams(
            collective_id=0, has_side_effects=True, vmem_limit_bytes=56 * 2**20
        ),
        name="transformer_block",
    )(
        latent,
        ln_gain[0],
        ln_bias[0],
        w_qkv[0].transpose(1, 0, 2).reshape(3 * HD, width),
        w_out[0],
        w_gate[0].T,
        w_value[0].T,
        w_down[0],
    )


def solution(mesh):
    return jax.shard_map(
        per_device,
        mesh=mesh,
        in_specs=(
            P("rows", "cols", None),
            P(),
            P(),
            P(None, "cols", None, None),
            P(None, "cols", None),
            P(None, None, "cols"),
            P(None, None, "cols"),
            P(None, "cols", None),
        ),
        out_specs=P("rows", "cols", None),
        check_vma=False,
    )
```

time: 74.1 us -> 67.9 us (0.916); the launches traced: 74 us -> 66.7 us
  Pallas kernels: 72.4 us -> 65.1 us
    pallas_call x1, Pallas kernels: 72.4 us -> 65.1 us  [per_device(): pl.pallas_call(block_kernel, out_shape=jax.ShapeDtypeStruct(latent.shape,...]
where the time goes in v4:
time: 67.9 us; the launch traced here: 66.7 us
  Pallas kernels  65.1 us (96%)
  local copies, waits for them, and re-layouts  1.55 us (2%)
    pallas_call x1, Pallas kernels, per_device(): pl.pallas_call(block_kernel, out_shape=jax.ShapeDtypeStruct(latent.shape,...  65.1 us
    unnamed x1, local copies, waits for them, and re-layouts  1.55 us

profile of v4, /device:TPU:1, one launch (start us, length us, event | category | flops | bytes accessed | tf_op | source)
XLA Modules:
  0.0 66.7 jit_solution(10775625309347607561)
XLA Ops:
  0.0 65.1 %transformer_block.1 = bf16[8,4,1280]{2,1,0:T(4,128)(2,1)} custom-call(bf16[8,4,1280]{2,1,0:T(4,128)(2,1)} %latent.1, f32[2,1280]{1,0:T(2,128)} %bitcast.20, f32[2,1280]{1,0:T(2,128)} %bitcast.21, bf16[192,1280]{1,0:T(8,128)(2,1)} %bitcast.18, bf16[64,1280]{1,0:T(8,128)(2,1)} %bitcast.19, bf16[320,1280]{1,0:T(8,128)(2,1)} %bitcast.15, ...), custom_call_target="tpu_custom_call" | custom-call | tf_op jit(solution)/shard_map/transformer_block/pallas_call | solution.py:349
  65.1 1.6 %copy.10 = bf16[8,4,1280]{2,1,0:T(4,128)(2,1)} copy(bf16[8,4,1280]{2,1,0:T(4,128)(2,1)} %transformer_block.1) | data formatting | bytes 163840

commit v5 on v4

--- a/solution.py
+++ b/solution.py
@@ -29,8 +29,7 @@
     latent, gain_in, bias_in, w_qkv, w_out, w_gate, w_value, w_down, result,
     rows_in, rows_far, gain, bias, tokens, stream, partial, summed, keys, query,
     wkv, wq, wo, wgv, wgv_t, wdown, top, accum, attn_sum, attended, attended_other,
-    sem_l, sem_w, sem_ws, sem_wr, sem_os, sem_or, sem_fs, sem_fr, sem_xs, sem_xr, sem_ys, sem_yr,
-    sem_as, sem_ar, sem_zs, sem_zr, sem_gs, sem_gr, sem_cs, sem_cr, sem_ps, sem_pr,
+    sem_l, sem_w, sem_wr, sem_or, sem_xr, sem_yr, sem_ar, sem_zr, sem_gr, sem_cr, sem_pr, sem_s,
 ):
     row, col = lax.axis_index("rows"), lax.axis_index("cols")
     core, me = col % 2, col // 2
@@ -49,12 +48,11 @@
             src_ref=src, dst_ref=dst, send_sem=send, recv_sem=recv, device_id=device, device_id_type=MESH
         )
 
-    started = []
-
-    def begin(*args):
-        copy = remote(*args)
+    NEAR, ACROSS, FAR, SHARE, SHARE_FFN, NEAR_KEYS, FAR_KEYS, SIBLING, OUT, FORWARD, RETURN, HEADS, PIECE = range(13)
+
+    def begin(src, dst, kind, recv, device):
+        copy = remote(src, dst, sem_s.at[kind], recv, device)
         copy.start()
-        started.append(copy)
         return copy
 
     barrier = pltpu.get_barrier_semaphore()
@@ -64,8 +62,6 @@
     for distance in range(1, 4):
         pl.semaphore_signal(barrier, inc=1, device_id=plane(distance), device_id_type=MESH)
     pl.semaphore_signal(barrier, inc=1, device_id=sibling, device_id_type=MESH)
-
-    local = []
 
     def begin_local(src, dst, sem):
         copy = pltpu.make_async_copy(src, dst, sem)
@@ -85,45 +81,40 @@
         (w_value, wgv.at[2], wgv.at[3]),
         (w_down, wdown.at[0], wdown.at[1]),
     ]
+    groups = (0, 0, 1, 2, 2, 3)
 
     def fetch(first, last):
-        return [begin_local(homes[index][0], homes[index][1], sem_w.at[index]) for index in range(first, last)]
-
-    def share(first, last):
-        return [
-            begin(homes[index][0], homes[index][2], sem_ws.at[index], sem_wr.at[index], sibling)
-            for index in range(first, last)
-        ]
-
-    own_weights = fetch(0, 3)
+        for index in range(first, last):
+            begin_local(homes[index][0], homes[index][1], sem_w.at[groups[index]])
+
+    def share(first, last, kind):
+        for index in range(first, last):
+            begin(homes[index][0], homes[index][2], kind, sem_wr.at[groups[index]], sibling)
+
+    def wait_weights(group, whole):
+        pltpu.make_async_copy(whole, whole, sem_w.at[group]).wait()
+        remote(whole, whole, sem_s.at[SHARE], sem_wr.at[group], sibling).wait_recv()
+
+    fetch(0, 3)
     pl.semaphore_wait(barrier, 12)
 
     across = [
-        begin(latent.at[pl.ds(4 * part, 4)], rows_far.at[me, part], sem_ps.at[part], sem_pr.at[part], plane(4))
+        begin(latent.at[pl.ds(4 * part, 4)], rows_far.at[me, part], ACROSS, sem_pr.at[part], plane(4))
         for part in range(2)
     ]
     for distance in range(7, 0, -1):
-        begin(latent, rows_in.at[me], sem_xs.at[distance], sem_xr.at[distance], chip(distance))
-    sent_weights = share(0, 3)
-
-    def spread_out(part, first, count):
-        return [
-            begin(
-                w_out.at[pl.ds(first, count)], wo.at[distance, mate, pl.ds(first, count)],
-                sem_os.at[part, distance], sem_or.at[part, distance], chip(distance),
-            )
-            for distance in range(7, 0, -1)
-        ]
-
-    copies_out = spread_out(0, 0, 16)
+        begin(latent, rows_in.at[me], NEAR, sem_xr.at[distance], chip(distance))
+    share(0, 3, SHARE)
+    fetch(3, 6)
+    share(3, 6, SHARE_FFN)
 
     def near_copy(distance):
         block = rows_in.at[lax.bitwise_xor(me, distance)]
-        return remote(block, block, sem_xs.at[distance], sem_xr.at[distance], chip(distance))
+        return remote(block, block, sem_s.at[NEAR], sem_xr.at[distance], chip(distance))
 
     def far_copy(part, distance):
         block = rows_far.at[lax.bitwise_xor(me, distance), part]
-        return remote(block, block, sem_ys.at[part, distance], sem_yr.at[part, distance], chip(distance))
+        return remote(block, block, sem_s.at[FAR], sem_yr.at[part, distance], chip(distance))
 
     def near_norm(distance):
         slot = lax.bitwise_xor(me, distance)
@@ -144,13 +135,9 @@
         across[part].wait_recv()
         for distance in range(7, 0, -1):
             mine = rows_far.at[me, part]
-            begin(mine, mine, sem_ys.at[part, distance], sem_yr.at[part, distance], chip(distance))
-    own_weights += fetch(3, 6)
-    sent_weights += share(3, 6)
+            begin(mine, mine, FAR, sem_yr.at[part, distance], chip(distance))
     lax.fori_loop(1, 8, near_step, 0)
-    for index in range(2):
-        own_weights[index].wait()
-        sent_weights[index].wait_recv()
+    wait_weights(0, w_qkv)
 
     scale = HD ** (-0.5) * math.log2(math.e)
 
@@ -162,31 +149,22 @@
 
     def send_sibling(slot):
         block = keys.at[slot, core]
-        return remote(block, block, sem_gs.at[slot], sem_gr.at[slot], sibling)
-
-    def from_sibling(slot):
-        block = keys.at[slot, 1 - core]
-        return remote(block, block, sem_gs.at[slot], sem_gr.at[slot], sibling)
-
-    def from_plane(slot, part):
-        block = keys.at[slot, core, pl.ds(128 * part, 128)]
-        return remote(block, block, sem_zs.at[slot, part], sem_zr.at[slot, part], plane(4))
+        begin(block, block, SIBLING, sem_gr.at[slot // 4], sibling)
+
+    def from_sibling(group):
+        blocks = keys.at[pl.ds(4 * group, 4), 1 - core]
+        remote(blocks, blocks, sem_s.at[SIBLING], sem_gr.at[group], sibling).wait_recv()
+
+    def from_plane(slot):
+        block = keys.at[slot, core]
+        remote(block, block, sem_s.at[NEAR_KEYS], sem_zr.at[slot], plane(4)).wait_recv()
 
     for part in range(2):
         project(0, part)
     for distance in range(3, 0, -1):
-        begin(
-            keys.at[0, core], keys.at[distance, core],
-            sem_zs.at[distance, 0], sem_zr.at[distance, 0], plane(distance),
-        )
-    send_sibling(0).start()
+        begin(keys.at[0, core], keys.at[distance, core], NEAR_KEYS, sem_zr.at[distance], plane(distance))
+    send_sibling(0)
     query[HD:, :] = jnp.zeros((HD, 512), BF16)
-    own_weights[3].wait()
-    own_weights[4].wait()
-    sent_weights[3].wait_recv()
-    sent_weights[4].wait_recv()
-    for index in range(4):
-        wgv_t[:, pl.ds(320 * index, 320)] = wgv[index].T
 
     def far_step(distance, part):
         @pl.when(distance >= 1)
@@ -205,10 +183,12 @@
         for distance in range(3, 0, -1):
             begin(
                 keys.at[4, core, place], keys.at[4 + distance, core, place],
-                sem_zs.at[4 + distance, part], sem_zr.at[4 + distance, part], plane(distance),
+                FAR_KEYS, sem_zr.at[4 + distance], plane(distance),
             )
-    send_sibling(4).start()
-    copies_out += spread_out(1, 16, 48)
+        if part == 0:
+            for distance in range(7, 0, -1):
+                begin(w_out, wo.at[distance, mate], OUT, sem_or.at[distance], chip(distance))
+    send_sibling(4)
 
     def scored(block, first, count):
         return dot(block, query[:, first : first + count], 1, 0)
@@ -229,68 +209,58 @@
         return (accum[HD:, first : first + 256] / accum[0:1, first : first + 256]).astype(BF16)
 
     for near in range(1, 4):
-        block = keys.at[near, core]
-        remote(block, block, sem_zs.at[near, 0], sem_zr.at[near, 0], plane(near)).wait_recv()
-        send_sibling(near).start()
-    for near in range(4):
-        from_sibling(near).wait_recv()
+        from_plane(near)
+        send_sibling(near)
+    wait_weights(2, wgv.at[pl.ds(0, 2)])
+    for index in range(4):
+        wgv_t[:, pl.ds(320 * index, 320)] = wgv[index].T
+    from_sibling(0)
     block = keys[0:4].reshape(2048, 2 * HD)
     scores = scored(block, 0, 512)
     first_top = jnp.max(scores, axis=0, keepdims=True)
     top[...] = first_top
     accum[...] = summed_values(block, jnp.exp2(scores - first_top).astype(BF16))
     for far in range(5, 8):
-        from_plane(far, 0).wait_recv()
-        from_plane(far, 1).wait_recv()
-        send_sibling(far).start()
+        from_plane(far)
+        send_sibling(far)
     fold(keys[pl.ds(4, 4), core].reshape(1024, 2 * HD), 256, 256)
-    for far in range(4, 8):
-        from_sibling(far).wait_recv()
+    from_sibling(1)
     fold(keys[pl.ds(4, 4), 1 - core].reshape(1024, 2 * HD), 256, 256)
     attended_other[...] = attended_by(256)
-    returned = begin(
-        attended_other, attended.at[0, pl.ds(HD, HD)], sem_ps.at[2], sem_pr.at[2], plane(4)
-    )
+    returned = begin(attended_other, attended.at[0, pl.ds(HD, HD)], RETURN, sem_pr.at[2], plane(4))
     fold(keys[4:8].reshape(2048, 2 * HD), 0, 256)
 
     attended[0, 0:HD] = attended_by(0)
-    copies = []
+    def spread_heads(part):
+        block = pl.ds(HD * part, HD)
+        for distance in range(7, 0, -1):
+            begin(
+                attended.at[0, block], attended.at[distance, block], HEADS, sem_ar.at[part], chip(distance)
+            )
+
+    def wait_heads(part):
+        blocks = attended.at[pl.ds(1, 7), pl.ds(HD * part, HD)]
+        remote(blocks, blocks, sem_s.at[HEADS], sem_ar.at[part], sibling).wait_recv()
+
+    spread_heads(0)
+    returned.wait_recv()
+    spread_heads(1)
+    wait_weights(1, w_out)
     for distance in range(7, 0, -1):
-        copies.append(
-            begin(
-                attended.at[0, pl.ds(0, HD)], attended.at[distance, pl.ds(0, HD)],
-                sem_as.at[0, distance], sem_ar.at[0, distance], chip(distance),
-            )
-        )
-    returned.wait_recv()
-    for distance in range(7, 0, -1):
-        copies.append(
-            begin(
-                attended.at[0, pl.ds(HD, HD)], attended.at[distance, pl.ds(HD, HD)],
-                sem_as.at[1, distance], sem_ar.at[1, distance], chip(distance),
-            )
-        )
-    own_weights[2].wait()
-    sent_weights[2].wait_recv()
-    forwarded = []
-    for index, distance in enumerate(range(7, 0, -1)):
-        copies_out[index].wait_recv()
-        copies_out[7 + index].wait_recv()
-        begin(wo.at[distance, mate], wo.at[distance, mate], sem_fs.at[distance], sem_fr.at[distance], sibling)
-        theirs = wo.at[distance, 1 - mate]
-        forwarded.append(remote(theirs, theirs, sem_fs.at[distance], sem_fr.at[distance], sibling))
-    for copy in forwarded + copies[:7]:
-        copy.wait_recv()
+        block = wo.at[distance, mate]
+        remote(block, block, sem_s.at[OUT], sem_or.at[distance], chip(distance)).wait_recv()
+        begin(block, block, FORWARD, sem_or.at[0], sibling)
+    blocks = wo.at[pl.ds(1, 7), 1 - mate]
+    remote(blocks, blocks, sem_s.at[FORWARD], sem_or.at[0], sibling).wait_recv()
+    wait_heads(0)
 
     def projected(part):
         heads = attended[:, HD * part : HD * (part + 1)].reshape(8 * HD, 256)
         return dot(heads, wo[:, part].reshape(8 * HD, width), 0, 0)
 
     attn_sum[...] = projected(0)
-    own_weights[5].wait()
-    sent_weights[5].wait_recv()
-    for copy in copies[7:]:
-        copy.wait_recv()
+    wait_weights(3, w_down)
+    wait_heads(1)
     total = stream[...].reshape(256, width).astype(F32) + (attn_sum[...] + projected(1))
     stream[...] = total.astype(BF16).reshape(stream.shape)
 
@@ -298,7 +268,7 @@
 
     def piece(slot):
         return remote(
-            partial.at[:, lax.bitwise_xor(me, slot)], summed.at[slot], sem_cs.at[slot], sem_cr.at[slot], chip(slot)
+            partial.at[:, lax.bitwise_xor(me, slot)], summed.at[slot], sem_s.at[PIECE], sem_cr.at[slot], chip(slot)
         )
 
     def feed(index, carry):
@@ -326,19 +296,24 @@
         total += summed[distance].astype(F32)
     result[...] = total.reshape(8, 4, width).astype(BF16)
 
-    for copy in started:
-        copy.wait_send()
-
-    def finish(slot, carry):
-        send_sibling(slot).wait_send()
-
-        @pl.when(slot >= 1)
-        def _():
-            piece(slot).wait_send()
-
-        return carry
-
-    lax.fori_loop(0, 8, finish, 0)
+    seven = pl.ds(0, 7)
+    three = keys.at[pl.ds(0, 3), 0]
+    for kind, sent in (
+        (NEAR, rows_in.at[seven]),
+        (ACROSS, rows_far.at[0]),
+        (FAR, rows_far.at[seven]),
+        (SHARE, wkv),
+        (SHARE_FFN, wgv.at[pl.ds(0, 3)]),
+        (NEAR_KEYS, three),
+        (FAR_KEYS, three),
+        (SIBLING, keys.at[:, 0]),
+        (OUT, wo.at[seven, 0]),
+        (FORWARD, wo.at[seven, 0]),
+        (RETURN, attended_other),
+        (HEADS, attended.at[seven]),
+        (PIECE, summed.at[seven]),
+    ):
+        remote(sent, sent, sem_s.at[kind], sem_pr.at[0], sibling).wait_send()
 
 
 def per_device(latent, ln_gain, ln_bias, w_qkv, w_out, w_gate, w_value, w_down):
@@ -348,7 +323,7 @@
     dma = pltpu.SemaphoreType.DMA
     return pl.pallas_call(
         block_kernel,
-        out_shape=jax.ShapeDtypeStruct(latent.shape, BF16),
+        out_shape=pltpu.VMEM(latent.shape, BF16),
         in_specs=[anywhere] * 8,
         out_specs=vmem,
         scratch_shapes=[
@@ -374,27 +349,17 @@
             pltpu.VMEM((8, 2 * HD, 256), BF16),
             pltpu.VMEM((HD, 256), BF16),
             dma((3,)),
-            dma((6,)),
-            dma((6,)),
-            dma((6,)),
-            dma((2, 8)),
-            dma((2, 8)),
-            dma((8,)),
-            dma((8,)),
+            dma((4,)),
+            dma((4,)),
             dma((8,)),
             dma((8,)),
             dma((2, 8)),
-            dma((2, 8)),
-            dma((2, 8)),
-            dma((2, 8)),
-            dma((8, 2)),
-            dma((8, 2)),
+            dma((2,)),
             dma((8,)),
-            dma((8,)),
-            dma((8,)),
+            dma((2,)),
             dma((8,)),
             dma((3,)),
-            dma((3,)),
+            dma((13,)),
         ],
         compiler_params=pltpu.CompilerParams(
             collective_id=0, has_side_effects=True, vmem_limit_bytes=56 * 2**20

time: 67.9 us -> 68.1 us (level); the launches traced: 66.7 us -> 68 us
  Pallas kernels: 65.1 us -> 67.4 us
  local copies, waits for them, and re-layouts: 1.55 us -> 0.64 us
    pallas_call x1, Pallas kernels: 65.1 us -> 67.4 us  [per_device(): pl.pallas_call(block_kernel, out_shape=pltpu.VMEM(latent.shape, BF16), in...]
    unnamed x1, local copies, waits for them, and re-layouts: 1.55 us -> 0.64 us
where the time goes in v5:
time: 68.1 us; the launch traced here: 68 us
  Pallas kernels  67.4 us (99%)
    pallas_call x1, Pallas kernels, per_device(): pl.pallas_call(block_kernel, out_shape=pltpu.VMEM(latent.shape, BF16), in...  67.4 us

profile of v5, /device:TPU:1, one launch (start us, length us, event | category | flops | bytes accessed | tf_op | source)
XLA Modules:
  0.0 68.0 jit_solution(4448194177248805806)
XLA Ops:
  0.0 67.4 %transformer_block.1 = bf16[8,4,1280]{2,1,0:T(4,128)(2,1)S(1)} custom-call(bf16[8,4,1280]{2,1,0:T(4,128)(2,1)} %latent.1, f32[2,1280]{1,0:T(2,128)} %bitcast.20, f32[2,1280]{1,0:T(2,128)} %bitcast.21, bf16[192,1280]{1,0:T(8,128)(2,1)} %bitcast.18, bf16[64,1280]{1,0:T(8,128)(2,1)} %bitcast.19, bf16[320,1280]{1,0:T(8,128)(2,1)} %bitcast.15, ...), custom_call_target="tpu_custom_call" | custom-call | tf_op jit(solution)/shard_map/transformer_block/pallas_call | solution.py:324
  67.4 0.6 copy.10

commit v6 on v5

--- a/solution.py
+++ b/solution.py
@@ -108,6 +108,12 @@
     fetch(3, 6)
     share(3, 6, SHARE_FFN)
 
+    def spread_out(rows):
+        for distance in range(7, 0, -1):
+            begin(w_out.at[rows], wo.at[distance, mate, rows], OUT, sem_or.at[distance], chip(distance))
+
+    spread_out(pl.ds(0, 16))
+
     def near_copy(distance):
         block = rows_in.at[lax.bitwise_xor(me, distance)]
         return remote(block, block, sem_s.at[NEAR], sem_xr.at[distance], chip(distance))
@@ -185,10 +191,8 @@
                 keys.at[4, core, place], keys.at[4 + distance, core, place],
                 FAR_KEYS, sem_zr.at[4 + distance], plane(distance),
             )
-        if part == 0:
-            for distance in range(7, 0, -1):
-                begin(w_out, wo.at[distance, mate], OUT, sem_or.at[distance], chip(distance))
     send_sibling(4)
+    spread_out(pl.ds(16, 48))
 
     def scored(block, first, count):
         return dot(block, query[:, first : first + count], 1, 0)

time: 68.1 us -> 63.9 us (0.938)
  Pallas kernels: 67.4 us -> 62.7 us
    pallas_call x1, Pallas kernels: 67.4 us -> 62.7 us  [per_device(): pl.pallas_call(block_kernel, out_shape=pltpu.VMEM(latent.shape, BF16), in...]
where the time goes in v6:
time: 63.9 us; the launch traced here: 63.3 us
  Pallas kernels  62.7 us (98%)
  local copies, waits for them, and re-layouts  0.64 us (1%)
    pallas_call x1, Pallas kernels, per_device(): pl.pallas_call(block_kernel, out_shape=pltpu.VMEM(latent.shape, BF16), in...  62.7 us

profile of v6, /device:TPU:1, one launch (start us, length us, event | category | flops | bytes accessed | tf_op | source)
XLA Modules:
  0.0 63.3 jit_solution(16361683145983820433)
XLA Ops:
  0.0 62.7 %transformer_block.1 = bf16[8,4,1280]{2,1,0:T(4,128)(2,1)S(1)} custom-call(bf16[8,4,1280]{2,1,0:T(4,128)(2,1)} %latent.1, f32[2,1280]{1,0:T(2,128)} %bitcast.20, f32[2,1280]{1,0:T(2,128)} %bitcast.21, bf16[192,1280]{1,0:T(8,128)(2,1)} %bitcast.18, bf16[64,1280]{1,0:T(8,128)(2,1)} %bitcast.19, bf16[320,1280]{1,0:T(8,128)(2,1)} %bitcast.15, ...), custom_call_target="tpu_custom_call" | custom-call | tf_op jit(solution)/shard_map/transformer_block/pallas_call | solution.py:328
  62.7 0.6 %copy.10 = bf16[8,4,1280]{2,1,0:T(4,128)(2,1)} copy(bf16[8,4,1280]{2,1,0:T(4,128)(2,1)S(1)} %transformer_block.1) | data formatting | bytes 163840

commit v7 on v6

--- a/solution.py
+++ b/solution.py
@@ -48,7 +48,7 @@
             src_ref=src, dst_ref=dst, send_sem=send, recv_sem=recv, device_id=device, device_id_type=MESH
         )
 
-    NEAR, ACROSS, FAR, SHARE, SHARE_FFN, NEAR_KEYS, FAR_KEYS, SIBLING, OUT, FORWARD, RETURN, HEADS, PIECE = range(13)
+    NEAR, ACROSS, FAR, SHARE, SHARE_FFN, NEAR_KEYS, FAR_KEYS, SIBLING, OUT, FORWARD, RETURN, HEADS, PIECE, EXCHANGE = range(14)
 
     def begin(src, dst, kind, recv, device):
         copy = remote(src, dst, sem_s.at[kind], recv, device)
@@ -98,9 +98,12 @@
     fetch(0, 3)
     pl.semaphore_wait(barrier, 12)
 
+    def quarter(slot, index):
+        return rows_far.at[slot, index // 2, pl.ds(2 * (index % 2), 2)]
+
     across = [
-        begin(latent.at[pl.ds(4 * part, 4)], rows_far.at[me, part], ACROSS, sem_pr.at[part], plane(4))
-        for part in range(2)
+        begin(latent.at[pl.ds(2 * index, 2)], quarter(me, index), ACROSS, sem_pr.at[index], plane(4))
+        for index in range(4)
     ]
     for distance in range(7, 0, -1):
         begin(latent, rows_in.at[me], NEAR, sem_xr.at[distance], chip(distance))
@@ -112,8 +115,6 @@
         for distance in range(7, 0, -1):
             begin(w_out.at[rows], wo.at[distance, mate, rows], OUT, sem_or.at[distance], chip(distance))
 
-    spread_out(pl.ds(0, 16))
-
     def near_copy(distance):
         block = rows_in.at[lax.bitwise_xor(me, distance)]
         return remote(block, block, sem_s.at[NEAR], sem_xr.at[distance], chip(distance))
@@ -137,11 +138,12 @@
     for copy in local:
         copy.wait()
     near_norm(0)
-    for part in range(2):
-        across[part].wait_recv()
+    for index in range(4):
+        across[index].wait_recv()
         for distance in range(7, 0, -1):
-            mine = rows_far.at[me, part]
-            begin(mine, mine, FAR, sem_yr.at[part, distance], chip(distance))
+            mine = quarter(me, index)
+            begin(mine, mine, FAR, sem_yr.at[index // 2, distance], chip(distance))
+    spread_out(pl.ds(0, 16))
     lax.fori_loop(1, 8, near_step, 0)
     wait_weights(0, w_qkv)
 
@@ -231,24 +233,27 @@
     from_sibling(1)
     fold(keys[pl.ds(4, 4), 1 - core].reshape(1024, 2 * HD), 256, 256)
     attended_other[...] = attended_by(256)
-    returned = begin(attended_other, attended.at[0, pl.ds(HD, HD)], RETURN, sem_pr.at[2], plane(4))
+    returned = begin(attended_other, attended.at[0, pl.ds(HD, HD)], RETURN, sem_pr.at[4], plane(4))
     fold(keys[4:8].reshape(2048, 2 * HD), 0, 256)
 
     attended[0, 0:HD] = attended_by(0)
-    def spread_heads(part):
-        block = pl.ds(HD * part, HD)
+    def spread_heads(group, block):
         for distance in range(7, 0, -1):
-            begin(
-                attended.at[0, block], attended.at[distance, block], HEADS, sem_ar.at[part], chip(distance)
-            )
-
-    def wait_heads(part):
-        blocks = attended.at[pl.ds(1, 7), pl.ds(HD * part, HD)]
-        remote(blocks, blocks, sem_s.at[HEADS], sem_ar.at[part], sibling).wait_recv()
-
-    spread_heads(0)
+            begin(attended.at[0, *block], attended.at[distance, *block], HEADS, sem_ar.at[group], chip(distance))
+
+    def wait_heads(group, block):
+        blocks = attended.at[pl.ds(1, 7), *block]
+        remote(blocks, blocks, sem_s.at[HEADS], sem_ar.at[group], sibling).wait_recv()
+
+    first_heads = (pl.ds(0, HD), pl.ds(0, 256))
+
+    def later_heads(part):
+        return pl.ds(HD, HD), pl.ds(pl.multiple_of(128 * part, 128), 128)
+
+    spread_heads(0, first_heads)
     returned.wait_recv()
-    spread_heads(1)
+    for part in range(2):
+        spread_heads(1 + part, later_heads(part))
     wait_weights(1, w_out)
     for distance in range(7, 0, -1):
         block = wo.at[distance, mate]
@@ -256,47 +261,42 @@
         begin(block, block, FORWARD, sem_or.at[0], sibling)
     blocks = wo.at[pl.ds(1, 7), 1 - mate]
     remote(blocks, blocks, sem_s.at[FORWARD], sem_or.at[0], sibling).wait_recv()
-    wait_heads(0)
-
-    def projected(part):
-        heads = attended[:, HD * part : HD * (part + 1)].reshape(8 * HD, 256)
-        return dot(heads, wo[:, part].reshape(8 * HD, width), 0, 0)
-
-    attn_sum[...] = projected(0)
+    wait_heads(0, first_heads)
+
+    heads = attended[:, :HD].reshape(8 * HD, 256)
+    attn_sum[...] = dot(heads, wo[:, 0].reshape(8 * HD, width), 0, 0).reshape(attn_sum.shape)
     wait_weights(3, w_down)
-    wait_heads(1)
-    total = stream[...].reshape(256, width).astype(F32) + (attn_sum[...] + projected(1))
-    stream[...] = total.astype(BF16).reshape(stream.shape)
 
     units = wdown.shape[0] * wdown.shape[1]
 
-    def piece(slot):
+    def piece(slot, part):
         return remote(
-            partial.at[:, lax.bitwise_xor(me, slot)], summed.at[slot], sem_s.at[PIECE], sem_cr.at[slot], chip(slot)
+            partial.at[part, lax.bitwise_xor(me, slot)], summed.at[slot, part],
+            sem_s.at[PIECE], sem_cr.at[slot], chip(slot),
         )
 
-    def feed(index, carry):
-        base = 4 * lax.bitwise_xor(1 - index, me // 4)
-        rows = stream[:, pl.ds(base, 4)].reshape(128, width).astype(F32)
+    def feed(part, carry):
+        wait_heads(1 + part, later_heads(part))
+        heads = attended[:, HD:, pl.ds(pl.multiple_of(128 * part, 128), 128)].reshape(8 * HD, 128)
+        added = attn_sum[part] + dot(heads, wo[:, 1].reshape(8 * HD, width), 0, 0)
+        rounded = (stream[part].reshape(128, width).astype(F32) + added).astype(BF16)
+        stream[part] = rounded.reshape(8, 16, width)
+        rows = rounded.astype(F32)
         normed = norm_rows(rows, gain[1:2, :], bias[1:2, :])
         sums = dot(normed, wgv_t[...], 1, 0)
         gate, value = sums[:, :units], sums[:, units:]
         hidden = (value * (gate * (lax.erf(gate * (0.5**0.5)) + 1.0) * 0.5)).astype(BF16)
         terms = dot(hidden, wdown[...].reshape(units, width), 1, 0)
-        partial[:, pl.ds(base, 4)] = terms.astype(BF16).reshape(2, 4, 16, width)
-        for offset in range(3, -1, -1):
-            distance = 4 - 4 * index + offset
-
-            @pl.when(distance >= 1)
-            def _():
-                piece(distance).start()
-
+        partial[part] = terms.astype(BF16).reshape(8, 16, width)
+        for distance in range(7, 0, -1):
+            piece(distance, part).start()
         return carry
 
     lax.fori_loop(0, 2, feed, 0)
     total = stream[:, me].astype(F32) + partial[:, me].astype(F32)
     for distance in range(1, 8):
-        piece(distance).wait_recv()
+        block = summed.at[distance]
+        remote(block, block, sem_s.at[PIECE], sem_cr.at[distance], sibling).wait_recv()
         total += summed[distance].astype(F32)
     result[...] = total.reshape(8, 4, width).astype(BF16)
 
@@ -349,7 +349,7 @@
             pltpu.VMEM((2, own_units, width), BF16),
             pltpu.VMEM((1, 512), F32),
             pltpu.VMEM((2 * HD, 512), F32),
-            pltpu.VMEM((256, width), F32),
+            pltpu.VMEM((2, 128, width), F32),
             pltpu.VMEM((8, 2 * HD, 256), BF16),
             pltpu.VMEM((HD, 256), BF16),
             dma((3,)),
@@ -358,12 +358,12 @@
             dma((8,)),
             dma((8,)),
             dma((2, 8)),
-            dma((2,)),
+            dma((3,)),
             dma((8,)),
             dma((2,)),
             dma((8,)),
-            dma((3,)),
-            dma((13,)),
+            dma((5,)),
+            dma((14,)),
         ],
         compiler_params=pltpu.CompilerParams(
             collective_id=0, has_side_effects=True, vmem_limit_bytes=56 * 2**20

time: 63.9 us -> 63.1 us (0.987)
  no operation moved by 1% of the time
where the time goes in v7:
time: 63.1 us; the launch traced here: 63 us
  Pallas kernels  62.3 us (99%)
  local copies, waits for them, and re-layouts  0.64 us (1%)
    pallas_call x1, Pallas kernels, per_device(): pl.pallas_call(block_kernel, out_shape=pltpu.VMEM(latent.shape, BF16), in...  62.3 us

profile of v7, /device:TPU:1, one launch (start us, length us, event | category | flops | bytes accessed | tf_op | source)
XLA Modules:
  0.0 63.0 jit_solution(2516484182248803678)
XLA Ops:
  0.0 62.3 %transformer_block.1 = bf16[8,4,1280]{2,1,0:T(4,128)(2,1)S(1)} custom-call(bf16[8,4,1280]{2,1,0:T(4,128)(2,1)} %latent.1, f32[2,1280]{1,0:T(2,128)} %bitcast.20, f32[2,1280]{1,0:T(2,128)} %bitcast.21, bf16[192,1280]{1,0:T(8,128)(2,1)} %bitcast.18, bf16[64,1280]{1,0:T(8,128)(2,1)} %bitcast.19, bf16[320,1280]{1,0:T(8,128)(2,1)} %bitcast.15, ...), custom_call_target="tpu_custom_call" | custom-call | tf_op jit(solution)/shard_map/transformer_block/pallas_call | solution.py:328
  62.4 0.6 %copy.10 = bf16[8,4,1280]{2,1,0:T(4,128)(2,1)} copy(bf16[8,4,1280]{2,1,0:T(4,128)(2,1)S(1)} %transformer_block.1) | data formatting | bytes 163840

commit v8 on v7

--- a/solution.py
+++ b/solution.py
@@ -96,17 +96,18 @@
         remote(whole, whole, sem_s.at[SHARE], sem_wr.at[group], sibling).wait_recv()
 
     fetch(0, 3)
+    local[0].wait()
     pl.semaphore_wait(barrier, 12)
 
     def quarter(slot, index):
         return rows_far.at[slot, index // 2, pl.ds(2 * (index % 2), 2)]
 
     across = [
-        begin(latent.at[pl.ds(2 * index, 2)], quarter(me, index), ACROSS, sem_pr.at[index], plane(4))
+        begin(rows_in.at[me, pl.ds(2 * index, 2)], quarter(me, index), ACROSS, sem_pr.at[index], plane(4))
         for index in range(4)
     ]
     for distance in range(7, 0, -1):
-        begin(latent, rows_in.at[me], NEAR, sem_xr.at[distance], chip(distance))
+        begin(rows_in.at[me], rows_in.at[me], NEAR, sem_xr.at[distance], chip(distance))
     share(0, 3, SHARE)
     fetch(3, 6)
     share(3, 6, SHARE_FFN)
@@ -135,7 +136,7 @@
         near_norm(distance)
         return carry
 
-    for copy in local:
+    for copy in local[1:]:
         copy.wait()
     near_norm(0)
     for index in range(4):
@@ -251,14 +252,14 @@
         return pl.ds(HD, HD), pl.ds(pl.multiple_of(128 * part, 128), 128)
 
     spread_heads(0, first_heads)
-    returned.wait_recv()
-    for part in range(2):
-        spread_heads(1 + part, later_heads(part))
     wait_weights(1, w_out)
     for distance in range(7, 0, -1):
         block = wo.at[distance, mate]
         remote(block, block, sem_s.at[OUT], sem_or.at[distance], chip(distance)).wait_recv()
         begin(block, block, FORWARD, sem_or.at[0], sibling)
+    returned.wait_recv()
+    for part in range(2):
+        spread_heads(1 + part, later_heads(part))
     blocks = wo.at[pl.ds(1, 7), 1 - mate]
     remote(blocks, blocks, sem_s.at[FORWARD], sem_or.at[0], sibling).wait_recv()
     wait_heads(0, first_heads)

time: 63.1 us -> 61.8 us (0.979)
  Pallas kernels: 62.3 us -> 61.1 us
    pallas_call x1, Pallas kernels: 62.3 us -> 61.1 us  [per_device(): pl.pallas_call(block_kernel, out_shape=pltpu.VMEM(latent.shape, BF16), in...]
where the time goes in v8:
time: 61.8 us; the launch traced here: 61.7 us
  Pallas kernels  61.1 us (99%)
  local copies, waits for them, and re-layouts  0.64 us (1%)
    pallas_call x1, Pallas kernels, per_device(): pl.pallas_call(block_kernel, out_shape=pltpu.VMEM(latent.shape, BF16), in...  61.1 us

profile of v8, /device:TPU:1, one launch (start us, length us, event | category | flops | bytes accessed | tf_op | source)
XLA Modules:
  0.0 61.7 jit_solution(16600845969279952415)
XLA Ops:
  0.0 61.1 %transformer_block.1 = bf16[8,4,1280]{2,1,0:T(4,128)(2,1)S(1)} custom-call(bf16[8,4,1280]{2,1,0:T(4,128)(2,1)} %latent.1, f32[2,1280]{1,0:T(2,128)} %bitcast.20, f32[2,1280]{1,0:T(2,128)} %bitcast.21, bf16[192,1280]{1,0:T(8,128)(2,1)} %bitcast.18, bf16[64,1280]{1,0:T(8,128)(2,1)} %bitcast.19, bf16[320,1280]{1,0:T(8,128)(2,1)} %bitcast.15, ...), custom_call_target="tpu_custom_call" | custom-call | tf_op jit(solution)/shard_map/transformer_block/pallas_call | solution.py:329
  61.1 0.6 %copy.10 = bf16[8,4,1280]{2,1,0:T(4,128)(2,1)} copy(bf16[8,4,1280]{2,1,0:T(4,128)(2,1)S(1)} %transformer_block.1) | data formatting | bytes 163840

commit v9 on v8

--- a/solution.py
+++ b/solution.py
@@ -144,8 +144,8 @@
         for distance in range(7, 0, -1):
             mine = quarter(me, index)
             begin(mine, mine, FAR, sem_yr.at[index // 2, distance], chip(distance))
+    lax.fori_loop(1, 8, near_step, 0)
     spread_out(pl.ds(0, 16))
-    lax.fori_loop(1, 8, near_step, 0)
     wait_weights(0, w_qkv)
 
     scale = HD ** (-0.5) * math.log2(math.e)
@@ -234,7 +234,15 @@
     from_sibling(1)
     fold(keys[pl.ds(4, 4), 1 - core].reshape(1024, 2 * HD), 256, 256)
     attended_other[...] = attended_by(256)
-    returned = begin(attended_other, attended.at[0, pl.ds(HD, HD)], RETURN, sem_pr.at[4], plane(4))
+    returned = []
+    for part in range(2):
+        place = pl.ds(128 * part, 128)
+        returned.append(
+            begin(
+                attended_other.at[:, place], attended.at[0, pl.ds(HD, HD), place],
+                RETURN, sem_pr.at[4 + part], plane(4),
+            )
+        )
     fold(keys[4:8].reshape(2048, 2 * HD), 0, 256)
 
     attended[0, 0:HD] = attended_by(0)
@@ -257,8 +265,8 @@
         block = wo.at[distance, mate]
         remote(block, block, sem_s.at[OUT], sem_or.at[distance], chip(distance)).wait_recv()
         begin(block, block, FORWARD, sem_or.at[0], sibling)
-    returned.wait_recv()
     for part in range(2):
+        returned[part].wait_recv()
         spread_heads(1 + part, later_heads(part))
     blocks = wo.at[pl.ds(1, 7), 1 - mate]
     remote(blocks, blocks, sem_s.at[FORWARD], sem_or.at[0], sibling).wait_recv()
@@ -363,7 +371,7 @@
             dma((8,)),
             dma((2,)),
             dma((8,)),
-            dma((5,)),
+            dma((6,)),
             dma((14,)),
         ],
         compiler_params=pltpu.CompilerParams(

time: 61.8 us -> 61.9 us (level)
  no operation moved by 1% of the time
where the time goes in v9:
time: 61.9 us; the launch traced here: 61.7 us
  Pallas kernels  61.1 us (99%)
  local copies, waits for them, and re-layouts  0.64 us (1%)
    pallas_call x1, Pallas kernels, per_device(): pl.pallas_call(block_kernel, out_shape=pltpu.VMEM(latent.shape, BF16), in...  61.1 us

profile of v9, /device:TPU:1, one launch (start us, length us, event | category | flops | bytes accessed | tf_op | source)
XLA Modules:
  0.0 61.7 jit_solution(6001671498171529045)
XLA Ops:
  0.0 61.1 %transformer_block.1 = bf16[8,4,1280]{2,1,0:T(4,128)(2,1)S(1)} custom-call(bf16[8,4,1280]{2,1,0:T(4,128)(2,1)} %latent.1, f32[2,1280]{1,0:T(2,128)} %bitcast.20, f32[2,1280]{1,0:T(2,128)} %bitcast.21, bf16[192,1280]{1,0:T(8,128)(2,1)} %bitcast.18, bf16[64,1280]{1,0:T(8,128)(2,1)} %bitcast.19, bf16[320,1280]{1,0:T(8,128)(2,1)} %bitcast.15, ...), custom_call_target="tpu_custom_call" | custom-call | tf_op jit(solution)/shard_map/transformer_block/pallas_call | solution.py:337
  61.1 0.6 %copy.10 = bf16[8,4,1280]{2,1,0:T(4,128)(2,1)} copy(bf16[8,4,1280]{2,1,0:T(4,128)(2,1)S(1)} %transformer_block.1) | data formatting | bytes 163840
